TPU v7x, 32 devices: a whole 2x2x4 slice. The times are simulated.
32 devices in a mesh: groups: 2 (over x), mesh: 16 (over z, y, core).
Axes of the slice: x: 2, y: 2, z: 4, core: 2. Of those that a mesh axis runs over, the one named last changes fastest.
Arguments:
- mesh_state: bfloat16 [128, 128, 512], P(('groups', 'mesh')), parts along dimension 0, may hold values from -8 to 8
- obs_latent: bfloat16 [1024, 128, 512], P(('groups', 'mesh')), parts along dimension 0, may hold values from -6 to 6
- pair_coupling: bfloat16 [1024, 128, 128], P(('groups', 'mesh')), parts along dimension 0, may hold values from -0.5 to 0.5
- pair_target: int32 [1024], P(('groups', 'mesh')), parts along dimension 0, may hold values from 0 to 11
- pair_source: int32 [1024], P(('groups', 'mesh')), parts along dimension 0, may hold values from 0 to 31
- pair_count: int32 [32], P(('groups', 'mesh')), parts along dimension 0, may hold values from 1 to 32, 256 in all
- mesh_coupling: bfloat16 [64, 4, 128, 128], P('mesh'), may hold values from -0.25 to 0.25
- neighbor: int32 [64, 4], P('mesh'), may hold values from 0 to 5, as said below
- rim_send: int32 [16, 2], P('mesh'), may hold values from 0 to 3, as said below
- enc_gain: float32 [512], replicated, may hold values from 0.25 to 1.75
- enc_self: bfloat16 [512, 512], replicated, may hold values from -0.25 to 0.25
- enc_obs: bfloat16 [512, 512], replicated, may hold values from -0.25 to 0.25
- enc_out: bfloat16 [512, 512], replicated, may hold values from -0.25 to 0.25
- node_gain: float32 [2, 512], replicated, may hold values from 0.25 to 1.75
- node_self: bfloat16 [2, 512, 512], replicated, may hold values from -0.25 to 0.25
- node_msg: bfloat16 [2, 512, 512], replicated, may hold values from -0.25 to 0.25
- node_out: bfloat16 [2, 512, 512], replicated, may hold values from -0.25 to 0.25
Outputs:
- mesh_out: bfloat16 [128, 128, 512], P(('groups', 'mesh')), parts along dimension 0
There are 2 independent parts, one for each index of `groups`. A program takes and returns all parts, laid end to end along the dimension named above; an argument that names none is the same for every part. Nothing has to cross between parts.
Inputs may be any that keep to these rules, and one draw needn't show every extreme that they name: pair_target // 4 - 1 is the offset (-1, 0 or 1) along mesh, modulo 16, from the pair's device to the device that owns the fed block; pair_target mod 4 is that block's local index there. `pair_source`: local observation block on the pair's own device. A device's live pairs are its first pair_count slots; some device has all 32 live. `neighbor`: values index a device's receive list: 0 the block from the left neighbour, 1 + c the local block c, 5 the block from the right neighbour; the entry at position 0 of each row is the block itself, the entry at position 1 lies before it in this list, the entry at position 2 after it. `rim_send`: two different local blocks of each device: the one sent to the left neighbour, then the one sent to the right.
All inputs are finite; a program needn't handle non-finite values.
Results may differ from a plain program's by a relative error of at most 0.014.
Values may be sent and summed in bfloat16 or wider, within the bound.
No kernel may reach another device: no remote copies, remote signals or barrier semaphores. Data moves between devices by JAX's collectives and lax.ppermute only.
A program may use at most 128 MiB of HBM per device.

v0:
```python
import jax
import jax.numpy as jnp
from jax import lax
from jax.experimental import pallas as pl
from jax.experimental.pallas import tpu as pltpu
from jax.sharding import PartitionSpec as P

F32 = jnp.float32
BF16 = jnp.bfloat16
VMEM = pl.BlockSpec(memory_space=pltpu.VMEM)
SMEM = pl.BlockSpec(memory_space=pltpu.SMEM)
HBM = pl.BlockSpec(memory_space=pltpu.HBM)


def dot(a, b):
    return jnp.dot(a, b, preferred_element_type=F32)


def silu(v):
    half = 0.5 * v
    return half + half * jnp.tanh(half)


def norm_rows(values, gain):
    center = values - jnp.mean(values, axis=-1, keepdims=True)
    spread = jnp.mean(center * center, axis=-1, keepdims=True)
    return (center * lax.rsqrt(spread + 1e-05) * gain).astype(BF16)


def odd_device():
    return lax.rem(lax.axis_index("mesh"), 2)


def pair_kernel(sides, cnt, tgt_hbm, src_hbm, obs, cpl, *refs):
    outs = refs[: len(sides)]
    tgt, src, listed, xbuf, cbuf, acc, isem, csem, xsem = refs[-9:]
    blocks, slots = outs[0].shape[0], xbuf.shape[0]
    odd = odd_device()
    parts = [{"off": 2 * odd, "on": 2 - 2 * odd, "self": 1}[side] for side in sides]
    reads = [
        pltpu.make_async_copy(tgt_hbm, tgt, isem.at[0]),
        pltpu.make_async_copy(src_hbm, src, isem.at[1]),
        pltpu.make_async_copy(cpl, cbuf, csem),
    ]
    for read in reads:
        read.start()
    reads[0].wait()
    reads[1].wait()
    groups = len(sides) * blocks

    def fetch(e, words):
        t = tgt[e]
        mine, group = jnp.bool_(False), jnp.int32(0)
        for i, part in enumerate(parts):
            here = (t >= part * blocks) & (t < (part + 1) * blocks)
            mine = mine | here
            group = jnp.where(here, t - part * blocks + i * blocks, group)
        word = words[0]
        for i in range(1, len(words)):
            word = jnp.where(group >= 4 * i, words[i], word)
        shift = 8 * (group & 3)

        @pl.when(mine)
        def _():
            pltpu.make_async_copy(obs.at[src[e]], xbuf.at[e], xsem.at[e]).start()
            listed[group * slots + ((word >> shift) & 255)] = e

        return [
            word + jnp.where(mine & (group >= 4 * i) & (group < 4 * i + 4), 1 << shift, 0)
            for i, word in enumerate(words)
        ]

    words = lax.fori_loop(0, cnt[0], fetch, [jnp.int32(0)] * (groups // 4))
    reads[2].wait()

    for g in range(groups):
        number = (words[g // 4] >> (8 * (g % 4))) & 255
        def some(first, n):
            at = [listed[g * slots + first + i] for i in range(n)]
            for e in at:
                pltpu.make_async_copy(obs.at[0], xbuf.at[e], xsem.at[e]).wait()
            left = jnp.concatenate([cbuf[e] for e in at], axis=1)
            right = jnp.concatenate([xbuf[e] for e in at], axis=0)
            return dot(left, right)

        @pl.when(number % 4 == 0)
        def _():
            acc[...] = jnp.zeros_like(acc)

        for n in range(1, 4):

            @pl.when(number % 4 == n)
            def _():
                acc[...] = some(0, n)

        def four(j, carry):
            acc[...] += some(number % 4 + 4 * j, 4)
            return carry

        lax.fori_loop(0, number // 4, four, 0)

        out = outs[g // blocks]
        out[g % blocks] = acc[...].astype(out.dtype)


def pair_sums(sides, blocks, tgt, src, cnt, obs, cpl, after=None):
    slots, rows, width = tgt.shape[0], obs.shape[1], obs.shape[2]
    more = [] if after is None else [after]
    return pl.pallas_call(
        lambda *refs: pair_kernel(list(sides), *refs[:5], *refs[5 + len(more) :]),
        out_shape=[jax.ShapeDtypeStruct((blocks, rows, width), d) for d in sides.values()],
        in_specs=[SMEM] + [HBM] * 4 + [pl.BlockSpec(memory_space=pl.ANY)] * len(more),
        out_specs=[VMEM] * len(sides),
        scratch_shapes=[
            pltpu.SMEM((slots,), jnp.int32),
            pltpu.SMEM((slots,), jnp.int32),
            pltpu.SMEM((len(sides) * blocks * slots,), jnp.int32),
            pltpu.VMEM((slots, rows, width), BF16),
            pltpu.VMEM((slots, rows, rows), BF16),
            pltpu.VMEM((rows, width), F32),
            pltpu.SemaphoreType.DMA((2,)),
            pltpu.SemaphoreType.DMA,
            pltpu.SemaphoreType.DMA((slots,)),
        ],
        compiler_params=pltpu.CompilerParams(vmem_limit_bytes=12 << 20),
        cost_estimate=pl.CostEstimate(flops=1 << 20, bytes_accessed=1 << 20, transcendentals=0),
        name="pairs_" + "_".join(sides),
    )(cnt, *[pltpu.with_memory_space_constraint(x, pltpu.HBM) for x in (tgt, src, obs, cpl)], *more)


def call(kernel, out, arrays, name, scalars=(), late=(), weight=20, place=VMEM, scratch=()):
    return pl.pallas_call(
        kernel,
        out_shape=out,
        in_specs=[SMEM] * len(scalars) + [pl.BlockSpec(memory_space=pl.ANY)] * len(late) + [VMEM] * len(arrays),
        out_specs=[place] * len(out),
        scratch_shapes=list(scratch),
        compiler_params=pltpu.CompilerParams(vmem_limit_bytes=14 << 20),
        cost_estimate=pl.CostEstimate(flops=1 << weight, bytes_accessed=1 << 20, transcendentals=0),
        name=name,
    )(*scalars, *late, *arrays)


def read_rim(rim_ref, rim, sem):
    copy = pltpu.make_async_copy(rim_ref, rim, sem)
    copy.start()

    def get():
        copy.wait()
        odd = odd_device()
        return rim[0, odd], rim[0, 1 - odd]

    return get


RIM = (pltpu.SMEM((1, 2), jnp.int32), pltpu.SemaphoreType.DMA)


def updates(states, pres, incoming, w_in, w_out):
    first = [dot(x, w_in) for x in incoming]
    hidden = [silu(p + x).astype(BF16) for p, x in zip(pres, first)]
    second = [dot(x, w_out) for x in hidden]
    return [(s.astype(F32) + x).astype(BF16) for s, x in zip(states, second)]


def prepare_kernel(nbr, state, gain, w_self, coupling, pre, mix):
    blocks, rows = state.shape[0], state.shape[1]
    odd = odd_device()
    last = blocks + 1
    codes = [1 + c for c in range(blocks)] + [last * odd, last - last * odd]
    for m in range(blocks):
        pre[m] = dot(norm_rows(state[m].astype(F32), gain[...]), w_self[...])
        for c, code in enumerate(codes):
            total = None
            for k in range(coupling.shape[1]):
                term = jnp.where(nbr[m, k] == code, coupling[m, k].astype(F32), 0.0)
                total = term if total is None else total + term
            mix[m, :, c * rows : (c + 1) * rows] = total.astype(BF16)


def encode_kernel(
    rim_ref, pre, base, own, on, off, w_obs, w_out, gain, mix, state, normed, rim_on, rim_off, packed, row, rim, sem
):
    blocks, rows, width = own.shape
    rims = read_rim(rim_ref, rim, sem)
    summed = [(own[m] + on[m].astype(F32) + off[m].astype(F32)).astype(BF16) for m in range(blocks)]
    each = range(blocks)
    updated = updates([base[m] for m in each], [pre[m] for m in each], summed, w_obs[...], w_out[...])
    for m in each:
        state[m] = updated[m]
        normed[m] = norm_rows(updated[m].astype(F32), gain[:1, :])
    off_rim, on_rim = rims()
    rim_on[...] = normed[on_rim]
    rim_off[...] = normed[off_rim]
    size = blocks * rows
    packed[:, :width] = state[off_rim]
    packed[:, width:] = mix[off_rim, :, size : size + rows]
    row[...] = mix[off_rim]


def part_kernel(row, normed, part):
    blocks, rows, width = normed.shape
    size = blocks * rows
    part[...] = dot(row[:, :size], normed[...].reshape(size, width))


def message_kernel(row, part, on, _, message):
    message[...] = (part[...] + dot(row[:, row.shape[1] - on.shape[0] :], on[...])).astype(BF16)


def neighbour_kernel(packed, rim_off, node_gain, n_self, _, state, normed, pre, message):
    rows, width = state.shape
    values = packed[:, :width]
    state[...] = values
    result = norm_rows(values.astype(F32), node_gain[:1, :])
    normed[...] = result
    pre[...] = dot(result, n_self[0])
    message[...] = dot(packed[:, width:], rim_off[...])


def round_kernel(rim_ref, mix, off, on, pre, heard, state, n_msg, n_out, gain, new_state, new_normed, rim_on, rim, sem):
    blocks, rows, width = state.shape
    rims = read_rim(rim_ref, rim, sem)
    size = blocks * rows
    sides = jnp.concatenate([off[...], on[...]], axis=0)
    each = range(blocks)
    incoming = [(heard[m] + dot(mix[m, :, size:], sides)).astype(BF16) for m in each]
    updated = updates([state[m] for m in each], [pre[m] for m in each], incoming, n_msg[0], n_out[0])
    for m in each:
        new_state[m] = updated[m]
        new_normed[m] = norm_rows(updated[m].astype(F32), gain[1:2, :])
    rim_on[...] = new_normed[rims()[1]]


def local_kernel(r, mix, normed, n_self, pre, message):
    blocks, rows, width = normed.shape
    size = blocks * rows
    own = normed[...].reshape(size, width)
    pre[...] = dot(own, n_self[r]).reshape(pre.shape)
    message[...] = dot(mix[...].reshape(size, -1)[:, :size], own).reshape(message.shape)


def far_kernel(arrived, far_message, pre, state, n_msg, n_out, gain, normed):
    incoming = (arrived[...].astype(F32) + far_message[...]).astype(BF16)
    (updated,) = updates([state[...]], [pre[...]], [incoming], n_msg[0], n_out[0])
    normed[...] = norm_rows(updated.astype(F32), gain[1:2, :])


def last_kernel(far, on, mix, pre, message, state, n_msg, n_out, out, stage, sems):
    blocks, rows, width = state.shape
    size = blocks * rows
    rims = jnp.concatenate([far[...], on[...]], axis=0)
    each = range(blocks)
    incoming = [(message[m] + dot(mix[m, :, size:], rims)).astype(BF16) for m in each]
    updated = updates([state[m] for m in each], [pre[m] for m in each], incoming, n_msg[1], n_out[1])
    copies = [pltpu.make_async_copy(stage.at[m], out.at[m], sems.at[m]) for m in each]
    for m in each:
        stage[m] = updated[m]
        copies[m].start()
    for copy in copies:
        copy.wait()


def shards(
    mesh_state,
    obs_latent,
    pair_coupling,
    pair_target,
    pair_source,
    pair_count,
    mesh_coupling,
    neighbor,
    rim_send,
    enc_gain,
    enc_self,
    enc_obs,
    enc_out,
    node_gain,
    node_self,
    node_msg,
    node_out,
):
    blocks, rows, width = mesh_state.shape
    size = blocks * rows
    count = lax.axis_size("mesh")
    on_route = [(i, i ^ 1) for i in range(count)]
    off_route = [(i, (i + 1) % count if i % 2 else (i - 1) % count) for i in range(count)]

    def swap_off(x):
        return lax.ppermute(x, "mesh", off_route)

    def swap_on(x):
        return lax.ppermute(x, "mesh", on_route)

    def shape(*dims, dtype=BF16):
        return jax.ShapeDtypeStruct(dims, dtype)

    whole, block = (blocks, rows, width), (rows, width)
    pairs = (pair_target, pair_source, pair_count, obs_latent, pair_coupling)
    (sent,) = pair_sums({"off": BF16}, blocks, *pairs)
    sums_off = swap_off(sent)
    sent_on, sums_own = pair_sums({"on": BF16, "self": F32}, blocks, *pairs, after=sent)
    sums_on = swap_on(sent_on)
    pre, mix = call(
        prepare_kernel,
        [shape(*whole, dtype=F32), shape(blocks, rows, size + 2 * rows)],
        [mesh_state, enc_gain[None], enc_self, mesh_coupling],
        "prepare",
        scalars=[neighbor],
        weight=34,
    )
    state, normed, rim_on, rim_off, packed, row = call(
        encode_kernel,
        [
            shape(*whole),
            shape(*whole),
            shape(*block),
            shape(*block),
            shape(rows, width + rows),
            shape(rows, size + 2 * rows),
        ],
        [pre, mesh_state, sums_own, sums_on, sums_off, enc_obs, enc_out, node_gain, mix],
        "encode",
        late=[rim_send],
        scratch=RIM,
    )
    packed = swap_off(packed)
    on = swap_on(rim_on)
    (part,) = call(part_kernel, [shape(*block, dtype=F32)], [row, normed], "rim_part")
    pre, heard = call(
        lambda *refs: local_kernel(0, *refs),
        [shape(*whole, dtype=F32), shape(*whole, dtype=F32)],
        [mix, normed, node_self],
        "round_0_local",
    )
    (message,) = call(message_kernel, [shape(*block)], [row, part, on, heard], "rim_message")
    arrived = swap_off(message)
    far_state, far, far_pre, far_message = call(
        neighbour_kernel,
        [shape(*block), shape(*block), shape(*block, dtype=F32), shape(*block, dtype=F32)],
        [packed, rim_off, node_gain, node_self, message],
        "neighbour_rim",
    )
    state, normed, rim_on = call(
        round_kernel,
        [shape(*whole), shape(*whole), shape(*block)],
        [mix, far, on, pre, heard, state, node_msg, node_out, node_gain],
        "round_0",
        late=[rim_send],
        scratch=RIM,
    )
    on = swap_on(rim_on)
    pre, message = call(
        lambda *refs: local_kernel(1, *refs),
        [shape(*whole, dtype=F32), shape(*whole, dtype=F32)],
        [mix, normed, node_self],
        "round_1_local",
    )
    (far,) = call(
        far_kernel,
        [shape(*block)],
        [arrived, far_message, far_pre, far_state, node_msg, node_out, node_gain],
        "far_rim",
    )
    (out,) = call(
        last_kernel,
        [shape(*whole)],
        [far, on, mix, pre, message, state, node_msg, node_out],
        "round_1",
        place=HBM,
        scratch=[pltpu.VMEM(whole, BF16), pltpu.SemaphoreType.DMA((blocks,))],
    )
    return out


def solution(mesh):
    block = P(("groups", "mesh"), None, None)
    return jax.shard_map(
        shards,
        mesh=mesh,
        in_specs=(
            block,
            block,
            block,
            P(("groups", "mesh")),
            P(("groups", "mesh")),
            P(("groups", "mesh")),
            P("mesh", None, None, None),
            P("mesh", None),
            P("mesh", None),
        )
        + (P(),) * 8,
        out_specs=block,
        check_vma=False,
    )
```

profile of v0, /device:TPU:0, one launch (start us, length us, event | category | flops | bytes accessed | tf_op | source)
XLA Modules:
  0.0 34.0 jit_solution(7245363990705441411)
XLA Ops:
  0.7 2.8 %pairs_off.1.refs_5_ = bf16[4,128,512]{2,1,0:T(8,128)(2,1)S(1)} custom-call(s32[1]{0:T(128)S(6)} %copy.18.refs_0_, s32[32]{0:T(128)} %refs_1_.3, s32[32]{0:T(128)} %refs_2_.5, bf16[32,128,512]{2,1,0:T(8,128)(2,1)} %refs_3_.3, bf16[32,128,128]{2,1,0:T(8,128)(2,1)} %refs_4_.3), custom_call_target="tpu_custom_call" | custom-call | flops 1048576 | bytes 1048576 | tf_op jit(solution)/shard_map/pairs_off/pallas_call | solution.py:109
  3.5 0.0 copy-start.3
  3.5 0.0 copy-start.8
  3.5 0.0 copy-start.9
  3.5 0.0 copy-start.10
  3.5 0.0 copy-start.11
  3.6 5.9 %collective-permute-start.1 = (bf16[4,128,512]{2,1,0:T(8,128)(2,1)S(1)}, bf16[4,128,512]{2,1,0:T(8,128)(2,1)S(1)}, u32[]{:S(2)}, u32[]{:S(2)}) collective-permute-start(bf16[4,128,512]{2,1,0:T(8,128)(2,1)S(1)} %pairs_off.1.refs_5_), channel_id=1, source_target_pairs={{0,15},{1,2},{2,1},{3,4},{4,3},{5,6},{6,5},{7,8},{8,7},{9,10},{10,... | collective-permute-start | bytes 1572872 | tf_op jit(solution)/shard_map/ppermute | solution.py:290
  9.5 4.0 %pairs_on_self.1 = (bf16[4,128,512]{2,1,0:T(8,128)(2,1)S(1)}, f32[4,128,512]{2,1,0:T(8,128)S(1)}) custom-call(s32[1]{0:T(128)S(6)} %copy.18.refs_0_, s32[32]{0:T(128)} %refs_1_.3, s32[32]{0:T(128)} %refs_2_.5, bf16[32,128,512]{2,1,0:T(8,128)(2,1)} %refs_3_.3, bf16[32,128,128]{2,1,0:T(8,128)(2,1)} %refs_4_.3, bf16[4,128,512]{2,1,0:T(8,128)(2,1)S(1)} %pairs_off.1.refs_5_), custom_call_target="tpu_custom_call" | custom-call | flops 1048576 | bytes 1048576 | tf_op jit(solution)/shard_map/pairs_on_self/pallas_call | solution.py:109
  13.5 0.1 collective-permute-start
  13.6 0.0 copy-start.4
  13.6 0.0 copy-start.5
  13.7 0.0 copy-start.6
  13.7 0.0 copy-start.7
  13.7 1.8 %prepare.1 = (f32[4,128,512]{2,1,0:T(8,128)S(1)}, bf16[4,128,768]{2,1,0:T(8,128)(2,1)S(1)}) custom-call(s32[4,4]{1,0:T(4,128)S(1)} %copy-done.10, bf16[4,128,512]{2,1,0:T(8,128)(2,1)S(1)} %copy-done.3, f32[1,512]{1,0:T(1,128)S(1)} %bitcast.1, bf16[512,512]{1,0:T(8,128)(2,1)S(1)} %copy-done.8, bf16[4,4,128,128]{3,2,1,0:T(8,128)(2,1)S(1)} %copy-done.9), custom_call_target="tpu_custom_call" | custom-call | flops 17179869184 | bytes 1048576 | tf_op jit(solution)/shard_map/prepare/pallas_call | solution.py:132
  15.5 0.0 copy-start
  15.5 0.9 %collective-permute-done.1.off = bf16[4,128,512]{2,1,0:T(8,128)(2,1)S(1)} collective-permute-done((bf16[4,128,512]{2,1,0:T(8,128)(2,1)S(1)}, bf16[4,128,512]{2,1,0:T(8,128)(2,1)S(1)}, u32[]{:S(2)}, u32[]{:S(2)}) %collective-permute-start.1) | collective-permute-done | bytes 524320 | tf_op jit(solution)/shard_map/ppermute | solution.py:290
  16.5 1.3 %encode.1 = (bf16[4,128,512]{2,1,0:T(8,128)(2,1)S(1)}, bf16[4,128,512]{2,1,0:T(8,128)(2,1)S(1)}, bf16[128,512]{1,0:T(8,128)(2,1)S(1)}, bf16[128,512]{1,0:T(8,128...) custom-call(s32[1,2]{1,0:T(1,128)S(1)} %copy-done.7, f32[4,128,512]{2,1,0:T(8,128)S(1)} %get-tuple-element.26.pre, ...), custom_call_target="tpu_custom_call" | custom-call | flops 1048576 | bytes 1048576 | tf_op jit(solution)/shard_map/encode/pallas_call | solution.py:132
  17.8 0.0 copy-start.1
  17.8 0.0 copy-start.2
  17.9 4.5 %collective-permute-start.4 = (bf16[128,640]{1,0:T(8,128)(2,1)S(1)}, bf16[128,640]{1,0:T(8,128)(2,1)S(1)}, u32[]{:S(2)}, u32[]{:S(2)}) collective-permute-start(bf16[128,640]{1,0:T(8,128)(2,1)S(1)} %get-tuple-element.34), channel_id=1, source_target_pairs={{0,15},{1,2},{2,1},{3,4},{4,3},{5,6},{6,5},{7,8},{8,7},{9,10},{10,... | collective-permute-start | bytes 491528 | tf_op jit(solution)/shard_map/ppermute | solution.py:290
  22.4 0.2 rim_part.1.part
  22.6 0.7 %round_0_local.1 = (f32[4,128,512]{2,1,0:T(8,128)S(1)}, f32[4,128,512]{2,1,0:T(8,128)S(1)}) custom-call(bf16[4,128,768]{2,1,0:T(8,128)(2,1)S(1)} %get-tuple-element.29.mix.refs_0_, bf16[4,128,512]{2,1,0:T(8,128)(2,1)S(1)} %get-tuple-element.31.normed.refs_1_, bf16[2,512,512]{2,1,0:T(8,128)(2,1)S(1)} %copy-done), custom_call_target="tpu_custom_call" | custom-call | flops 1048576 | bytes 1048576 | tf_op jit(solution)/shard_map/round_0_local/pallas_call | solution.py:132
  23.3 0.4 %collective-permute-done.2.on = bf16[128,512]{1,0:T(8,128)(2,1)S(1)} collective-permute-done((bf16[128,512]{1,0:T(8,128)(2,1)S(1)}, bf16[128,512]{1,0:T(8,128)(2,1)S(1)}, u32[]{:S(2)}, u32[]{:S(2)}) %collective-permute-start.2) | collective-permute-done | bytes 131104 | tf_op jit(solution)/shard_map/ppermute | solution.py:293
  23.7 0.2 rim_message.1._
  23.9 5.2 %collective-permute-start.3 = (bf16[128,512]{1,0:T(8,128)(2,1)S(1)}, bf16[128,512]{1,0:T(8,128)(2,1)S(1)}, u32[]{:S(2)}, u32[]{:S(2)}) collective-permute-start(bf16[128,512]{1,0:T(8,128)(2,1)S(1)} %rim_message.1._), channel_id=1, source_target_pairs={{0,15},{1,2},{2,1},{3,4},{4,3},{5,6},{6,5},{7,8},{8,7},{9,10},{10,... | collective-permute-start | bytes 393224 | tf_op jit(solution)/shard_map/ppermute | solution.py:290
  29.1 0.4 %neighbour_rim.1 = (bf16[128,512]{1,0:T(8,128)(2,1)S(1)}, bf16[128,512]{1,0:T(8,128)(2,1)S(1)}, f32[128,512]{1,0:T(8,128)S(1)}, f32[128,512]{1,0:T(8,128)S(1)}) custom-call(bf16[128,640]{1,0:T(8,128)(2,1)S(1)} %collective-permute-done.4.packed, bf16[128,512]{1,0:T(8,128)(2,1)S(1)} %get-tuple-element.35.rim_off, f32[2,512]{1,0:T(2,128)S(1)} %copy-done.6, ...), custom_call_target="tpu_custom_call" | custom-call | flops 1048576 | bytes 1048576 | tf_op jit(solution)/shard_map/neighbour_rim/pallas_call | solution.py:132
  29.5 1.2 %round_0.1 = (bf16[4,128,512]{2,1,0:T(8,128)(2,1)S(1)}, bf16[4,128,512]{2,1,0:T(8,128)(2,1)S(1)}, bf16[128,512]{1,0:T(8,128)(2,1)S(1)}) custom-call(s32[1,2]{1,0:T(1,128)S(1)} %copy-done.7, bf16[4,128,768]{2,1,0:T(8,128)(2,1)S(1)} %get-tuple-element.29.mix.refs_0_, bf16[128,512]{1,0:T(8,128)(2,1)S(1)} %get-tuple-element.39.off, ...), custom_call_target="tpu_custom_call" | custom-call | flops 1048576 | bytes 1048576 | tf_op jit(solution)/shard_map/round_0/pallas_call | solution.py:132
  30.7 0.1 collective-permute-start.5
  30.8 0.7 %round_1_local.1 = (f32[4,128,512]{2,1,0:T(8,128)S(1)}, f32[4,128,512]{2,1,0:T(8,128)S(1)}) custom-call(bf16[4,128,768]{2,1,0:T(8,128)(2,1)S(1)} %get-tuple-element.29.mix.refs_0_, bf16[4,128,512]{2,1,0:T(8,128)(2,1)S(1)} %get-tuple-element.43.refs_1_, bf16[2,512,512]{2,1,0:T(8,128)(2,1)S(1)} %copy-done), custom_call_target="tpu_custom_call" | custom-call | flops 1048576 | bytes 1048576 | tf_op jit(solution)/shard_map/round_1_local/pallas_call | solution.py:132
  31.5 0.2 collective-permute-done.3.arrived
  31.7 0.6 %far_rim.1.far = bf16[128,512]{1,0:T(8,128)(2,1)S(1)} custom-call(bf16[128,512]{1,0:T(8,128)(2,1)S(1)} %collective-permute-done.3.arrived, f32[128,512]{1,0:T(8,128)S(1)} %get-tuple-element.36.far_message, f32[128,512]{1,0:T(8,128)S(1)} %get-tuple-element.37.pre, bf16[128,512]{1,0:T(8,128)(2,1)S(1)} %get-tuple-element.38.state, ...), custom_call_target="tpu_custom_call" | custom-call | flops 1048576 | bytes 1048576 | tf_op jit(solution)/shard_map/far_rim/pallas_call | solution.py:132
  32.4 1.6 %round_1.1 = bf16[4,128,512]{2,1,0:T(8,128)(2,1)} custom-call(bf16[128,512]{1,0:T(8,128)(2,1)S(1)} %far_rim.1.far, bf16[128,512]{1,0:T(8,128)(2,1)S(1)} %collective-permute-done.5.on, bf16[4,128,768]{2,1,0:T(8,128)(2,1)S(1)} %get-tuple-element.29.mix.refs_0_, f32[4,128,512]{2,1,0:T(8,128)S(1)} %get-tuple-element.44.pre, ...), custom_call_target="tpu_custom_call" | custom-call | flops 1048576 | bytes 1048576 | tf_op jit(solution)/shard_map/round_1/pallas_call | solution.py:132
  (16 shorter events, 0.0 us)
Async XLA Ops:
  3.5 10.1 %copy-start.3 = (bf16[4,128,512]{2,1,0:T(8,128)(2,1)S(1)}, bf16[4,128,512]{2,1,0:T(8,128)(2,1)}, u32[]{:S(2)}) copy-start(bf16[4,128,512]{2,1,0:T(8,128)(2,1)} %base.1) | copy-start | bytes 1572868
  3.5 10.1 %copy-start.8 = (bf16[512,512]{1,0:T(8,128)(2,1)S(1)}, bf16[512,512]{1,0:T(8,128)(2,1)}, u32[]{:S(2)}) copy-start(bf16[512,512]{1,0:T(8,128)(2,1)} %w_self.1) | copy-start | bytes 1572868
  3.5 10.1 %copy-start.9 = (bf16[4,4,128,128]{3,2,1,0:T(8,128)(2,1)S(1)}, bf16[4,4,128,128]{3,2,1,0:T(8,128)(2,1)}, u32[]{:S(2)}) copy-start(bf16[4,4,128,128]{3,2,1,0:T(8,128)(2,1)} %coupling.1) | copy-start | bytes 1572868
  3.5 10.1 %copy-start.10 = (s32[4,4]{1,0:T(4,128)S(1)}, s32[4,4]{1,0:T(4,128)}, u32[]{:S(2)}) copy-start(s32[4,4]{1,0:T(4,128)} %nbr.1) | copy-start | bytes 196
  3.5 10.1 %copy-start.11 = (f32[512]{0:T(512)S(1)}, f32[512]{0:T(512)}, u32[]{:S(2)}) copy-start(f32[512]{0:T(512)} %param.26) | copy-start | bytes 6148
  3.6 12.9 %collective-permute-start.1 = (bf16[4,128,512]{2,1,0:T(8,128)(2,1)S(1)}, bf16[4,128,512]{2,1,0:T(8,128)(2,1)S(1)}, u32[]{:S(2)}, u32[]{:S(2)}) collective-permute-start(bf16[4,128,512]{2,1,0:T(8,128)(2,1)S(1)} %pairs_off.1.refs_5_), channel_id=1, source_target_pairs={{0,15},{1,2},{2,1},{3,4},{4,3},{5,6},{6,5},{7,8},{8,7},{9,10},{10,... | collective-permute-start | bytes 1572872 | tf_op jit(solution)/shard_map/ppermute | solution.py:290
  13.5 2.0 %collective-permute-start = (bf16[4,128,512]{2,1,0:T(8,128)(2,1)S(1)}, bf16[4,128,512]{2,1,0:T(8,128)(2,1)S(1)}, u32[]{:S(2)}, u32[]{:S(2)}) collective-permute-start(bf16[4,128,512]{2,1,0:T(8,128)(2,1)S(1)} %get-tuple-element.28), channel_id=1, source_target_pairs={{0,1},{1,0},{2,3},{3,2},{4,5},{5,4},{6,7},{7,6},{8,9},{9,8},{10,11... | collective-permute-start | bytes 1572872 | tf_op jit(solution)/shard_map/ppermute | solution.py:293
  13.6 2.8 %copy-start.4 = (bf16[512,512]{1,0:T(8,128)(2,1)S(1)}, bf16[512,512]{1,0:T(8,128)(2,1)}, u32[]{:S(2)}) copy-start(bf16[512,512]{1,0:T(8,128)(2,1)} %w_obs.1) | copy-start | bytes 1572868
  13.6 2.8 %copy-start.5 = (bf16[512,512]{1,0:T(8,128)(2,1)S(1)}, bf16[512,512]{1,0:T(8,128)(2,1)}, u32[]{:S(2)}) copy-start(bf16[512,512]{1,0:T(8,128)(2,1)} %w_out.1) | copy-start | bytes 1572868
  13.7 2.8 %copy-start.6 = (f32[2,512]{1,0:T(2,128)S(1)}, f32[2,512]{1,0:T(2,128)}, u32[]{:S(2)}) copy-start(f32[2,512]{1,0:T(2,128)} %gain.5) | copy-start | bytes 12292
  13.7 2.8 %copy-start.7 = (s32[1,2]{1,0:T(1,128)S(1)}, s32[1,2]{1,0:T(1,128)}, u32[]{:S(2)}) copy-start(s32[1,2]{1,0:T(1,128)} %rim_ref.3) | copy-start | bytes 28
  15.5 7.1 %copy-start = (bf16[2,512,512]{2,1,0:T(8,128)(2,1)S(1)}, bf16[2,512,512]{2,1,0:T(8,128)(2,1)}, u32[]{:S(2)}) copy-start(bf16[2,512,512]{2,1,0:T(8,128)(2,1)} %refs_2_.7) | copy-start | bytes 3145732
  17.8 11.7 %copy-start.1 = (bf16[2,512,512]{2,1,0:T(8,128)(2,1)S(1)}, bf16[2,512,512]{2,1,0:T(8,128)(2,1)}, u32[]{:S(2)}) copy-start(bf16[2,512,512]{2,1,0:T(8,128)(2,1)} %n_msg.5) | copy-start | bytes 3145732
  17.8 11.6 %copy-start.2 = (bf16[2,512,512]{2,1,0:T(8,128)(2,1)S(1)}, bf16[2,512,512]{2,1,0:T(8,128)(2,1)}, u32[]{:S(2)}) copy-start(bf16[2,512,512]{2,1,0:T(8,128)(2,1)} %n_out.5) | copy-start | bytes 3145732
  17.9 11.2 %collective-permute-start.4 = (bf16[128,640]{1,0:T(8,128)(2,1)S(1)}, bf16[128,640]{1,0:T(8,128)(2,1)S(1)}, u32[]{:S(2)}, u32[]{:S(2)}) collective-permute-start(bf16[128,640]{1,0:T(8,128)(2,1)S(1)} %get-tuple-element.34), channel_id=1, source_target_pairs={{0,15},{1,2},{2,1},{3,4},{4,3},{5,6},{6,5},{7,8},{8,7},{9,10},{10,... | collective-permute-start | bytes 491528 | tf_op jit(solution)/shard_map/ppermute | solution.py:290
  22.4 1.3 %collective-permute-start.2 = (bf16[128,512]{1,0:T(8,128)(2,1)S(1)}, bf16[128,512]{1,0:T(8,128)(2,1)S(1)}, u32[]{:S(2)}, u32[]{:S(2)}) collective-permute-start(bf16[128,512]{1,0:T(8,128)(2,1)S(1)} %get-tuple-element.32), channel_id=1, source_target_pairs={{0,1},{1,0},{2,3},{3,2},{4,5},{5,4},{6,7},{7,6},{8,9},{9,8},{10,11... | collective-permute-start | bytes 393224 | tf_op jit(solution)/shard_map/ppermute | solution.py:293
  23.9 7.8 %collective-permute-start.3 = (bf16[128,512]{1,0:T(8,128)(2,1)S(1)}, bf16[128,512]{1,0:T(8,128)(2,1)S(1)}, u32[]{:S(2)}, u32[]{:S(2)}) collective-permute-start(bf16[128,512]{1,0:T(8,128)(2,1)S(1)} %rim_message.1._), channel_id=1, source_target_pairs={{0,15},{1,2},{2,1},{3,4},{4,3},{5,6},{6,5},{7,8},{8,7},{9,10},{10,... | collective-permute-start | bytes 393224 | tf_op jit(solution)/shard_map/ppermute | solution.py:290
  30.7 1.6 %collective-permute-start.5 = (bf16[128,512]{1,0:T(8,128)(2,1)S(1)}, bf16[128,512]{1,0:T(8,128)(2,1)S(1)}, u32[]{:S(2)}, u32[]{:S(2)}) collective-permute-start(bf16[128,512]{1,0:T(8,128)(2,1)S(1)} %get-tuple-element.42), channel_id=1, source_target_pairs={{0,1},{1,0},{2,3},{3,2},{4,5},{5,4},{6,7},{7,6},{8,9},{9,8},{10,11... | collective-permute-start | bytes 393224 | tf_op jit(solution)/shard_map/ppermute | solution.py:293
where the time goes:
time: 33.7 us; the launch traced here: 34 us
  starting transfers between devices  15.8 us (47%)
  Pallas kernels  15.7 us (47%)
  waiting for transfers between devices  1.52 us (5%)
  between operations  0.93 us (3%)
    ppermute x3, starting transfers between devices, swap_off(): return lax.ppermute(x, 'mesh', off_route)  15.6 us
    pallas_call x10, Pallas kernels, call(): pl.pallas_call(kernel, out_shape=out, in_specs=[SMEM] * len(scalars) + [p...  8.85 us
    pallas_call x2, Pallas kernels, pair_sums(): pl.pallas_call(lambda *refs: pair_kernel(list(sides), *refs[:5], *refs[5...  6.84 us
    ppermute x3, waiting for transfers between devices, swap_off(): return lax.ppermute(x, 'mesh', off_route)  1.12 us
  transfers between devices with their start and end apart: 6, of which 3 were waited for; matrix products, arithmetic and copies ran while one was open for 0% of the time, Pallas kernels for 29%

commit v1 on v0

--- a/solution.py
+++ b/solution.py
@@ -31,12 +31,21 @@
     return lax.rem(lax.axis_index("mesh"), 2)
 
 
-def pair_kernel(sides, cnt, tgt_hbm, src_hbm, obs, cpl, *refs):
+def early_device():
+    me, count = lax.axis_index("mesh"), lax.axis_size("mesh")
+    return (me == 0) | ((lax.rem(me, 2) == 1) & (me != count - 1))
+
+
+def pair_kernel(sides, blocks, cnt, tgt_hbm, src_hbm, obs, cpl, *refs):
     outs = refs[: len(sides)]
     tgt, src, listed, xbuf, cbuf, acc, isem, csem, xsem = refs[-9:]
-    blocks, slots = outs[0].shape[0], xbuf.shape[0]
+    slots = xbuf.shape[0]
     odd = odd_device()
-    parts = [{"off": 2 * odd, "on": 2 - 2 * odd, "self": 1}[side] for side in sides]
+    rows_of = {"off": 2 * odd, "on": 2 - 2 * odd, "self": 1}
+    lows = [rows_of[side[0]] * blocks + side[1] for side in sides]
+    highs = [low + jnp.where(early_device(), side[2], side[4]) for low, side in zip(lows, sides)]
+    sizes = [side[2] for side in sides]
+    starts = [sum(sizes[:i]) for i in range(len(sizes))]
     reads = [
         pltpu.make_async_copy(tgt_hbm, tgt, isem.at[0]),
         pltpu.make_async_copy(src_hbm, src, isem.at[1]),
@@ -46,15 +55,15 @@
         read.start()
     reads[0].wait()
     reads[1].wait()
-    groups = len(sides) * blocks
+    groups = sum(sizes)
 
     def fetch(e, words):
         t = tgt[e]
-        mine, group = jnp.bool_(False), jnp.int32(0)
-        for i, part in enumerate(parts):
-            here = (t >= part * blocks) & (t < (part + 1) * blocks)
+        live, mine, group = e < cnt[0], jnp.bool_(False), jnp.int32(0)
+        for low, high, start in zip(lows, highs, starts):
+            here = live & (t >= low) & (t < high)
             mine = mine | here
-            group = jnp.where(here, t - part * blocks + i * blocks, group)
+            group = jnp.where(here, t - low + start, group)
         word = words[0]
         for i in range(1, len(words)):
             word = jnp.where(group >= 4 * i, words[i], word)
@@ -70,7 +79,7 @@
             for i, word in enumerate(words)
         ]
 
-    words = lax.fori_loop(0, cnt[0], fetch, [jnp.int32(0)] * (groups // 4))
+    words = lax.fori_loop(0, slots, fetch, [jnp.int32(0)] * pl.cdiv(groups, 4), unroll=8)
     reads[2].wait()
 
     for g in range(groups):
@@ -99,22 +108,33 @@
 
         lax.fori_loop(0, number // 4, four, 0)
 
-        out = outs[g // blocks]
-        out[g % blocks] = acc[...].astype(out.dtype)
-
-
-def pair_sums(sides, blocks, tgt, src, cnt, obs, cpl, after=None):
+        side = max(i for i, start in enumerate(starts) if start <= g)
+        outs[side][g - starts[side]] = acc[...].astype(outs[side].dtype)
+
+
+def pair_sums(sides, blocks, tgt, src, cnt, obs, cpl, after=(), late_only=False):
     slots, rows, width = tgt.shape[0], obs.shape[1], obs.shape[2]
-    more = [] if after is None else [after]
+    more = list(after)
+
+    def kernel(*refs):
+        def run():
+            pair_kernel(sides, blocks, *refs[:5], *refs[5 + len(more) :])
+
+        if late_only:
+            pl.when(jnp.logical_not(early_device()))(run)
+        else:
+            run()
+
     return pl.pallas_call(
-        lambda *refs: pair_kernel(list(sides), *refs[:5], *refs[5 + len(more) :]),
-        out_shape=[jax.ShapeDtypeStruct((blocks, rows, width), d) for d in sides.values()],
-        in_specs=[SMEM] + [HBM] * 4 + [pl.BlockSpec(memory_space=pl.ANY)] * len(more),
+        kernel,
+        input_output_aliases={5: 0} if late_only else {},
+        out_shape=[jax.ShapeDtypeStruct((side[2], rows, width), side[3]) for side in sides],
+        in_specs=[SMEM] + [HBM] * 4 + [VMEM if late_only and i == 0 else pl.BlockSpec(memory_space=pl.ANY) for i in range(len(more))],
         out_specs=[VMEM] * len(sides),
         scratch_shapes=[
             pltpu.SMEM((slots,), jnp.int32),
             pltpu.SMEM((slots,), jnp.int32),
-            pltpu.SMEM((len(sides) * blocks * slots,), jnp.int32),
+            pltpu.SMEM((sum(side[2] for side in sides) * slots,), jnp.int32),
             pltpu.VMEM((slots, rows, width), BF16),
             pltpu.VMEM((slots, rows, rows), BF16),
             pltpu.VMEM((rows, width), F32),
@@ -124,7 +144,7 @@
         ],
         compiler_params=pltpu.CompilerParams(vmem_limit_bytes=12 << 20),
         cost_estimate=pl.CostEstimate(flops=1 << 20, bytes_accessed=1 << 20, transcendentals=0),
-        name="pairs_" + "_".join(sides),
+        name="pairs_" + "_".join(side[0] for side in sides) + ("_late" if late_only else ""),
     )(cnt, *[pltpu.with_memory_space_constraint(x, pltpu.HBM) for x in (tgt, src, obs, cpl)], *more)
 
 
@@ -170,25 +190,40 @@
     codes = [1 + c for c in range(blocks)] + [last * odd, last - last * odd]
     for m in range(blocks):
         pre[m] = dot(norm_rows(state[m].astype(F32), gain[...]), w_self[...])
+        before, after, other = [coupling[m, k] for k in range(1, 4)]
+        zero = jnp.zeros_like(other)
         for c, code in enumerate(codes):
-            total = None
-            for k in range(coupling.shape[1]):
-                term = jnp.where(nbr[m, k] == code, coupling[m, k].astype(F32), 0.0)
-                total = term if total is None else total + term
-            mix[m, :, c * rows : (c + 1) * rows] = total.astype(BF16)
-
-
-def encode_kernel(
-    rim_ref, pre, base, own, on, off, w_obs, w_out, gain, mix, state, normed, rim_on, rim_off, packed, row, rim, sem
+            total = jnp.where(nbr[m, 3] == code, other, zero)
+            if c == m:
+                total = total + coupling[m, 0]
+            if c < m or c >= blocks:
+                total = total + jnp.where(nbr[m, 1] == code, before, zero)
+            if c > m:
+                total = total + jnp.where(nbr[m, 2] == code, after, zero)
+            mix[m, :, c * rows : (c + 1) * rows] = total
+
+
+def encode_kernel(first, pre, base, own, on, off, w_obs, w_out, gain, state, normed):
+    number = off.shape[0]
+    each = range(first, first + number)
+    summed = [(own[m] + on[m].astype(F32) + off[m - first].astype(F32)).astype(BF16) for m in each]
+    updated = updates([base[m] for m in each], [pre[m] for m in each], summed, w_obs[...], w_out[...])
+    for i in range(number):
+        state[i] = updated[i]
+        normed[i] = norm_rows(updated[i].astype(F32), gain[:1, :])
+
+
+def encode_rest_kernel(
+    rim_ref, pre, base, own, on, off, w_obs, w_out, gain, state_a, normed_a, mix,
+    state, normed, rim_on, rim_off, packed, row, rim, sem,
 ):
     blocks, rows, width = own.shape
+    half = blocks - off.shape[0]
     rims = read_rim(rim_ref, rim, sem)
-    summed = [(own[m] + on[m].astype(F32) + off[m].astype(F32)).astype(BF16) for m in range(blocks)]
-    each = range(blocks)
-    updated = updates([base[m] for m in each], [pre[m] for m in each], summed, w_obs[...], w_out[...])
-    for m in each:
-        state[m] = updated[m]
-        normed[m] = norm_rows(updated[m].astype(F32), gain[:1, :])
+    state[:half] = state_a[...]
+    normed[:half] = normed_a[...]
+    tail = pl.ds(half, blocks - half)
+    encode_kernel(half, pre, base, own, on, off, w_obs, w_out, gain, state.at[tail], normed.at[tail])
     off_rim, on_rim = rims()
     rim_on[...] = normed[on_rim]
     rim_off[...] = normed[off_rim]
@@ -297,9 +332,14 @@
 
     whole, block = (blocks, rows, width), (rows, width)
     pairs = (pair_target, pair_source, pair_count, obs_latent, pair_coupling)
-    (sent,) = pair_sums({"off": BF16}, blocks, *pairs)
-    sums_off = swap_off(sent)
-    sent_on, sums_own = pair_sums({"on": BF16, "self": F32}, blocks, *pairs, after=sent)
+    half = blocks // 2
+    rest = blocks - half
+    sent, sent_rest = pair_sums([("off", 0, half, BF16, half), ("off", half, rest, BF16, 0)], blocks, *pairs)
+    off_a = swap_off(sent)
+    (sent,) = pair_sums([("off", half, rest, BF16, rest)], blocks, *pairs, after=(sent_rest, sent), late_only=True)
+    off_b = swap_off(sent)
+    sides = [("on", 0, blocks, BF16, blocks), ("self", 0, blocks, F32, blocks)]
+    sent_on, sums_own = pair_sums(sides, blocks, *pairs, after=(sent,))
     sums_on = swap_on(sent_on)
     pre, mix = call(
         prepare_kernel,
@@ -309,8 +349,14 @@
         scalars=[neighbor],
         weight=34,
     )
+    encode = [pre, mesh_state, sums_own, sums_on]
+    weights = [enc_obs, enc_out, node_gain]
+    halves = [shape(half, rows, width), shape(half, rows, width)]
+    state, normed = call(
+        lambda *refs: encode_kernel(0, *refs), halves, [*encode, off_a, *weights], "encode_first"
+    )
     state, normed, rim_on, rim_off, packed, row = call(
-        encode_kernel,
+        encode_rest_kernel,
         [
             shape(*whole),
             shape(*whole),
@@ -319,8 +365,8 @@
             shape(rows, width + rows),
             shape(rows, size + 2 * rows),
         ],
-        [pre, mesh_state, sums_own, sums_on, sums_off, enc_obs, enc_out, node_gain, mix],
-        "encode",
+        [*encode, off_b, *weights, state, normed, mix],
+        "encode_rest",
         late=[rim_send],
         scratch=RIM,
     )

time: 33.7 us -> 33 us (0.979)
  starting transfers between devices: 15.8 us -> 12.5 us
  Pallas kernels: 15.7 us -> 17.3 us
  waiting for transfers between devices: 1.52 us -> 2.23 us
    ppermute x3 -> x4, starting transfers between devices: 15.6 us -> 12.4 us  [swap_off(): return lax.ppermute(x, 'mesh', off_route)]
    pallas_call x2 -> x3, Pallas kernels: 6.84 us -> 8.62 us  [pair_sums(): pl.pallas_call(kernel, input_output_aliases={5: 0} if late_only else {},...]
    ppermute x3 -> x4, waiting for transfers between devices: 1.12 us -> 1.52 us  [swap_off(): return lax.ppermute(x, 'mesh', off_route)]
    pallas_call x10 -> x11, Pallas kernels: 8.85 us -> 8.72 us  [call(): pl.pallas_call(kernel, out_shape=out, in_specs=[SMEM] * len(scalars) + [p...]
  transfers between devices with their start and end apart: 6 -> 7, of which waited for: 3 -> 3; matrix products, arithmetic and copies ran while one was open for 0% -> 0% of each run, Pallas kernels for 29% -> 35%
where the time goes in v1:
time: 33 us; the launch traced here: 33.1 us
  Pallas kernels  17.3 us (52%)
  starting transfers between devices  12.5 us (38%)
  waiting for transfers between devices  2.23 us (7%)
  between operations  0.96 us (3%)
    ppermute x4, starting transfers between devices, swap_off(): return lax.ppermute(x, 'mesh', off_route)  12.4 us
    pallas_call x11, Pallas kernels, call(): pl.pallas_call(kernel, out_shape=out, in_specs=[SMEM] * len(scalars) + [p...  8.72 us
    pallas_call x3, Pallas kernels, pair_sums(): pl.pallas_call(kernel, input_output_aliases={5: 0} if late_only else {},...  8.62 us
    ppermute x4, waiting for transfers between devices, swap_off(): return lax.ppermute(x, 'mesh', off_route)  1.52 us
    ppermute x3, waiting for transfers between devices, swap_on(): return lax.ppermute(x, 'mesh', on_route)  0.7 us
  transfers between devices with their start and end apart: 7, of which 3 were waited for; matrix products, arithmetic and copies ran while one was open for 0% of the time, Pallas kernels for 35%

profile of v1, /device:TPU:0, one launch (start us, length us, event | category | flops | bytes accessed | tf_op | source)
XLA Modules:
  0.0 33.1 jit_solution(12868054382333975129)
XLA Ops:
  0.7 3.3 %pairs_off_off.1 = (bf16[2,128,512]{2,1,0:T(8,128)(2,1)S(1)}, bf16[2,128,512]{2,1,0:T(8,128)(2,1)S(1)}) custom-call(s32[1]{0:T(128)S(6)} %copy.20.refs_0_, s32[32]{0:T(128)} %refs_1_.6, s32[32]{0:T(128)} %refs_2_.7, bf16[32,128,512]{2,1,0:T(8,128)(2,1)} %refs_3_.5, bf16[32,128,128]{2,1,0:T(8,128)(2,1)} %refs_4_.5), custom_call_target="tpu_custom_call" | custom-call | flops 1048576 | bytes 1048576 | tf_op jit(solution)/shard_map/pairs_off_off/pallas_call | solution.py:128
  4.0 5.0 %collective-permute-start.2 = (bf16[2,128,512]{2,1,0:T(8,128)(2,1)S(1)}, bf16[2,128,512]{2,1,0:T(8,128)(2,1)S(1)}, u32[]{:S(2)}, u32[]{:S(2)}) collective-permute-start(bf16[2,128,512]{2,1,0:T(8,128)(2,1)S(1)} %get-tuple-element.32.refs_6_), channel_id=1, source_target_pairs={{0,15},{1,2},{2,1},{3,4},{4,3},{5,6},{6,5},{7,8},{8,7},{9,10},{10,... | collective-permute-start | bytes 786440 | tf_op jit(solution)/shard_map/ppermute | solution.py:325
  9.0 0.3 pairs_off_late.1.refs_5_
  9.3 0.0 copy-start.3
  9.4 0.0 copy-start.8
  9.4 0.0 copy-start.9
  9.4 0.0 copy-start.10
  9.4 0.0 copy-start.11
  9.4 2.8 %collective-permute-start.1 = (bf16[2,128,512]{2,1,0:T(8,128)(2,1)S(1)}, bf16[2,128,512]{2,1,0:T(8,128)(2,1)S(1)}, u32[]{:S(2)}, u32[]{:S(2)}) collective-permute-start(bf16[2,128,512]{2,1,0:T(8,128)(2,1)S(1)} %pairs_off_late.1.refs_5_), channel_id=1, source_target_pairs={{0,15},{1,2},{2,1},{3,4},{4,3},{5,6},{6,5},{7,8},{8,7},{9,10},{10,... | collective-permute-start | bytes 786440 | tf_op jit(solution)/shard_map/ppermute | solution.py:325
  12.2 5.0 %pairs_on_self.1 = (bf16[4,128,512]{2,1,0:T(8,128)(2,1)S(1)}, f32[4,128,512]{2,1,0:T(8,128)S(1)}) custom-call(s32[1]{0:T(128)S(6)} %copy.20.refs_0_, s32[32]{0:T(128)} %refs_1_.6, s32[32]{0:T(128)} %refs_2_.7, bf16[32,128,512]{2,1,0:T(8,128)(2,1)} %refs_3_.5, bf16[32,128,128]{2,1,0:T(8,128)(2,1)} %refs_4_.5, bf16[2,128,512]{2,1,0:T(8,128)(2,1)S(1)} %pairs_off_late.1.refs_5_), custom_call_target="tpu_custom_call" | custom-call | flops 1048576 | bytes 1048576 | tf_op jit(solution)/shard_map/pairs_on_self/pallas_call | solution.py:128
  17.2 0.1 collective-permute-start
  17.3 0.0 copy-start.4
  17.3 0.0 copy-start.6
  17.3 1.5 %prepare.1 = (f32[4,128,512]{2,1,0:T(8,128)S(1)}, bf16[4,128,768]{2,1,0:T(8,128)(2,1)S(1)}) custom-call(s32[4,4]{1,0:T(4,128)S(1)} %copy-done.10, bf16[4,128,512]{2,1,0:T(8,128)(2,1)S(1)} %copy-done.3, f32[1,512]{1,0:T(1,128)S(1)} %bitcast.1, bf16[512,512]{1,0:T(8,128)(2,1)S(1)} %copy-done.8, bf16[4,4,128,128]{3,2,1,0:T(8,128)(2,1)S(1)} %copy-done.9), custom_call_target="tpu_custom_call" | custom-call | flops 17179869184 | bytes 1048576 | tf_op jit(solution)/shard_map/prepare/pallas_call | solution.py:152
  18.8 0.3 collective-permute-done.refs_3_.on
  19.1 0.7 %encode_first.1 = (bf16[2,128,512]{2,1,0:T(8,128)(2,1)S(1)}, bf16[2,128,512]{2,1,0:T(8,128)(2,1)S(1)}) custom-call(f32[4,128,512]{2,1,0:T(8,128)S(1)} %get-tuple-element.30.refs_0_.pre, bf16[4,128,512]{2,1,0:T(8,128)(2,1)S(1)} %copy-done.3, f32[4,128,512]{2,1,0:T(8,128)S(1)} %get-tuple-element.33.refs_2_.own, ...), custom_call_target="tpu_custom_call" | custom-call | flops 1048576 | bytes 1048576 | tf_op jit(solution)/shard_map/encode_first/pallas_call | solution.py:152
  19.9 0.0 copy-start
  19.9 0.8 %encode_rest.1 = (bf16[4,128,512]{2,1,0:T(8,128)(2,1)S(1)}, bf16[4,128,512]{2,1,0:T(8,128)(2,1)S(1)}, bf16[128,512]{1,0:T(8,128)(2,1)S(1)}, bf16[128,512]{1,0:T(...) custom-call(s32[1,2]{1,0:T(1,128)S(1)} %copy-done.7, ...), custom_call_target="tpu_custom_call" | custom-call | flops 1048576 | bytes 1048576 | tf_op jit(solution)/shard_map/encode_rest/pallas_call | solution.py:152
  20.7 0.0 copy-start.2
  20.8 0.9 %collective-permute-start.5 = (bf16[128,640]{1,0:T(8,128)(2,1)S(1)}, bf16[128,640]{1,0:T(8,128)(2,1)S(1)}, u32[]{:S(2)}, u32[]{:S(2)}) collective-permute-start(bf16[128,640]{1,0:T(8,128)(2,1)S(1)} %get-tuple-element.42), channel_id=1, source_target_pairs={{0,15},{1,2},{2,1},{3,4},{4,3},{5,6},{6,5},{7,8},{8,7},{9,10},{10,... | collective-permute-start | bytes 491528 | tf_op jit(solution)/shard_map/ppermute | solution.py:325
  21.6 0.2 rim_part.1.part
  21.9 0.7 %round_0_local.1 = (f32[4,128,512]{2,1,0:T(8,128)S(1)}, f32[4,128,512]{2,1,0:T(8,128)S(1)}) custom-call(bf16[4,128,768]{2,1,0:T(8,128)(2,1)S(1)} %get-tuple-element.37.mix.refs_0_, bf16[4,128,512]{2,1,0:T(8,128)(2,1)S(1)} %get-tuple-element.39.normed.refs_1_, bf16[2,512,512]{2,1,0:T(8,128)(2,1)S(1)} %copy-done), custom_call_target="tpu_custom_call" | custom-call | flops 1048576 | bytes 1048576 | tf_op jit(solution)/shard_map/round_0_local/pallas_call | solution.py:152
  22.6 0.4 %collective-permute-done.3.on = bf16[128,512]{1,0:T(8,128)(2,1)S(1)} collective-permute-done((bf16[128,512]{1,0:T(8,128)(2,1)S(1)}, bf16[128,512]{1,0:T(8,128)(2,1)S(1)}, u32[]{:S(2)}, u32[]{:S(2)}) %collective-permute-start.3) | collective-permute-done | bytes 131104 | tf_op jit(solution)/shard_map/ppermute | solution.py:328
  23.0 0.2 rim_message.1._
  23.2 3.7 %collective-permute-start.4 = (bf16[128,512]{1,0:T(8,128)(2,1)S(1)}, bf16[128,512]{1,0:T(8,128)(2,1)S(1)}, u32[]{:S(2)}, u32[]{:S(2)}) collective-permute-start(bf16[128,512]{1,0:T(8,128)(2,1)S(1)} %rim_message.1._), channel_id=1, source_target_pairs={{0,15},{1,2},{2,1},{3,4},{4,3},{5,6},{6,5},{7,8},{8,7},{9,10},{10,... | collective-permute-start | bytes 393224 | tf_op jit(solution)/shard_map/ppermute | solution.py:325
  26.8 1.5 %collective-permute-done.5.packed = bf16[128,640]{1,0:T(8,128)(2,1)S(1)} collective-permute-done((bf16[128,640]{1,0:T(8,128)(2,1)S(1)}, bf16[128,640]{1,0:T(8,128)(2,1)S(1)}, u32[]{:S(2)}, u32[]{:S(2)}) %collective-permute-start.5) | collective-permute-done | bytes 163872 | tf_op jit(solution)/shard_map/ppermute | solution.py:325
  28.4 0.4 %neighbour_rim.1 = (bf16[128,512]{1,0:T(8,128)(2,1)S(1)}, bf16[128,512]{1,0:T(8,128)(2,1)S(1)}, f32[128,512]{1,0:T(8,128)S(1)}, f32[128,512]{1,0:T(8,128)S(1)}) custom-call(bf16[128,640]{1,0:T(8,128)(2,1)S(1)} %collective-permute-done.5.packed, bf16[128,512]{1,0:T(8,128)(2,1)S(1)} %get-tuple-element.43.rim_off, f32[2,512]{1,0:T(2,128)S(1)} %copy-done.6, ...), custom_call_target="tpu_custom_call" | custom-call | flops 1048576 | bytes 1048576 | tf_op jit(solution)/shard_map/neighbour_rim/pallas_call | solution.py:152
  28.8 1.2 %round_0.1 = (bf16[4,128,512]{2,1,0:T(8,128)(2,1)S(1)}, bf16[4,128,512]{2,1,0:T(8,128)(2,1)S(1)}, bf16[128,512]{1,0:T(8,128)(2,1)S(1)}) custom-call(s32[1,2]{1,0:T(1,128)S(1)} %copy-done.7, bf16[4,128,768]{2,1,0:T(8,128)(2,1)S(1)} %get-tuple-element.37.mix.refs_0_, bf16[128,512]{1,0:T(8,128)(2,1)S(1)} %get-tuple-element.47.off, ...), custom_call_target="tpu_custom_call" | custom-call | flops 1048576 | bytes 1048576 | tf_op jit(solution)/shard_map/round_0/pallas_call | solution.py:152
  30.0 0.1 collective-permute-start.6
  30.1 0.7 %round_1_local.1 = (f32[4,128,512]{2,1,0:T(8,128)S(1)}, f32[4,128,512]{2,1,0:T(8,128)S(1)}) custom-call(bf16[4,128,768]{2,1,0:T(8,128)(2,1)S(1)} %get-tuple-element.37.mix.refs_0_, bf16[4,128,512]{2,1,0:T(8,128)(2,1)S(1)} %get-tuple-element.51.refs_1_, bf16[2,512,512]{2,1,0:T(8,128)(2,1)S(1)} %copy-done), custom_call_target="tpu_custom_call" | custom-call | flops 1048576 | bytes 1048576 | tf_op jit(solution)/shard_map/round_1_local/pallas_call | solution.py:152
  30.8 0.6 %far_rim.1.far = bf16[128,512]{1,0:T(8,128)(2,1)S(1)} custom-call(bf16[128,512]{1,0:T(8,128)(2,1)S(1)} %collective-permute-done.4.arrived, f32[128,512]{1,0:T(8,128)S(1)} %get-tuple-element.44.far_message, f32[128,512]{1,0:T(8,128)S(1)} %get-tuple-element.45.pre, bf16[128,512]{1,0:T(8,128)(2,1)S(1)} %get-tuple-element.46.state, ...), custom_call_target="tpu_custom_call" | custom-call | flops 1048576 | bytes 1048576 | tf_op jit(solution)/shard_map/far_rim/pallas_call | solution.py:152
  31.5 1.6 %round_1.1 = bf16[4,128,512]{2,1,0:T(8,128)(2,1)} custom-call(bf16[128,512]{1,0:T(8,128)(2,1)S(1)} %far_rim.1.far, bf16[128,512]{1,0:T(8,128)(2,1)S(1)} %collective-permute-done.6.on, bf16[4,128,768]{2,1,0:T(8,128)(2,1)S(1)} %get-tuple-element.37.mix.refs_0_, f32[4,128,512]{2,1,0:T(8,128)S(1)} %get-tuple-element.52.pre, ...), custom_call_target="tpu_custom_call" | custom-call | flops 1048576 | bytes 1048576 | tf_op jit(solution)/shard_map/round_1/pallas_call | solution.py:152
  (20 shorter events, 0.1 us)
Async XLA Ops:
  4.0 14.8 %collective-permute-start.2 = (bf16[2,128,512]{2,1,0:T(8,128)(2,1)S(1)}, bf16[2,128,512]{2,1,0:T(8,128)(2,1)S(1)}, u32[]{:S(2)}, u32[]{:S(2)}) collective-permute-start(bf16[2,128,512]{2,1,0:T(8,128)(2,1)S(1)} %get-tuple-element.32.refs_6_), channel_id=1, source_target_pairs={{0,15},{1,2},{2,1},{3,4},{4,3},{5,6},{6,5},{7,8},{8,7},{9,10},{10,... | collective-permute-start | bytes 786440 | tf_op jit(solution)/shard_map/ppermute | solution.py:325
  9.3 7.9 %copy-start.3 = (bf16[4,128,512]{2,1,0:T(8,128)(2,1)S(1)}, bf16[4,128,512]{2,1,0:T(8,128)(2,1)}, u32[]{:S(2)}) copy-start(bf16[4,128,512]{2,1,0:T(8,128)(2,1)} %base.1) | copy-start | bytes 1572868
  9.4 7.9 %copy-start.8 = (bf16[512,512]{1,0:T(8,128)(2,1)S(1)}, bf16[512,512]{1,0:T(8,128)(2,1)}, u32[]{:S(2)}) copy-start(bf16[512,512]{1,0:T(8,128)(2,1)} %w_self.1) | copy-start | bytes 1572868
  9.4 7.9 %copy-start.9 = (bf16[4,4,128,128]{3,2,1,0:T(8,128)(2,1)S(1)}, bf16[4,4,128,128]{3,2,1,0:T(8,128)(2,1)}, u32[]{:S(2)}) copy-start(bf16[4,4,128,128]{3,2,1,0:T(8,128)(2,1)} %coupling.1) | copy-start | bytes 1572868
  9.4 7.9 %copy-start.10 = (s32[4,4]{1,0:T(4,128)S(1)}, s32[4,4]{1,0:T(4,128)}, u32[]{:S(2)}) copy-start(s32[4,4]{1,0:T(4,128)} %nbr.1) | copy-start | bytes 196
  9.4 7.9 %copy-start.11 = (f32[512]{0:T(512)S(1)}, f32[512]{0:T(512)}, u32[]{:S(2)}) copy-start(f32[512]{0:T(512)} %param.26) | copy-start | bytes 6148
  9.4 10.5 %collective-permute-start.1 = (bf16[2,128,512]{2,1,0:T(8,128)(2,1)S(1)}, bf16[2,128,512]{2,1,0:T(8,128)(2,1)S(1)}, u32[]{:S(2)}, u32[]{:S(2)}) collective-permute-start(bf16[2,128,512]{2,1,0:T(8,128)(2,1)S(1)} %pairs_off_late.1.refs_5_), channel_id=1, source_target_pairs={{0,15},{1,2},{2,1},{3,4},{4,3},{5,6},{6,5},{7,8},{8,7},{9,10},{10,... | collective-permute-start | bytes 786440 | tf_op jit(solution)/shard_map/ppermute | solution.py:325
  17.2 2.0 %collective-permute-start = (bf16[4,128,512]{2,1,0:T(8,128)(2,1)S(1)}, bf16[4,128,512]{2,1,0:T(8,128)(2,1)S(1)}, u32[]{:S(2)}, u32[]{:S(2)}) collective-permute-start(bf16[4,128,512]{2,1,0:T(8,128)(2,1)S(1)} %get-tuple-element.34), channel_id=1, source_target_pairs={{0,1},{1,0},{2,3},{3,2},{4,5},{5,4},{6,7},{7,6},{8,9},{9,8},{10,11... | collective-permute-start | bytes 1572872 | tf_op jit(solution)/shard_map/ppermute | solution.py:328
  17.3 1.8 %copy-start.4 = (bf16[512,512]{1,0:T(8,128)(2,1)S(1)}, bf16[512,512]{1,0:T(8,128)(2,1)}, u32[]{:S(2)}) copy-start(bf16[512,512]{1,0:T(8,128)(2,1)} %w_obs.1) | copy-start | bytes 1572868
  17.3 1.8 %copy-start.5 = (bf16[512,512]{1,0:T(8,128)(2,1)S(1)}, bf16[512,512]{1,0:T(8,128)(2,1)}, u32[]{:S(2)}) copy-start(bf16[512,512]{1,0:T(8,128)(2,1)} %w_out.1) | copy-start | bytes 1572868
  17.3 1.8 %copy-start.6 = (f32[2,512]{1,0:T(2,128)S(1)}, f32[2,512]{1,0:T(2,128)}, u32[]{:S(2)}) copy-start(f32[2,512]{1,0:T(2,128)} %gain.5) | copy-start | bytes 12292
  18.8 1.1 %copy-start.7 = (s32[1,2]{1,0:T(1,128)S(1)}, s32[1,2]{1,0:T(1,128)}, u32[]{:S(2)}) copy-start(s32[1,2]{1,0:T(1,128)} %rim_ref.3) | copy-start | bytes 28
  19.9 2.0 %copy-start = (bf16[2,512,512]{2,1,0:T(8,128)(2,1)S(1)}, bf16[2,512,512]{2,1,0:T(8,128)(2,1)}, u32[]{:S(2)}) copy-start(bf16[2,512,512]{2,1,0:T(8,128)(2,1)} %refs_2_.9) | copy-start | bytes 3145732
  20.7 8.1 %copy-start.1 = (bf16[2,512,512]{2,1,0:T(8,128)(2,1)S(1)}, bf16[2,512,512]{2,1,0:T(8,128)(2,1)}, u32[]{:S(2)}) copy-start(bf16[2,512,512]{2,1,0:T(8,128)(2,1)} %n_msg.5) | copy-start | bytes 3145732
  20.7 8.1 %copy-start.2 = (bf16[2,512,512]{2,1,0:T(8,128)(2,1)S(1)}, bf16[2,512,512]{2,1,0:T(8,128)(2,1)}, u32[]{:S(2)}) copy-start(bf16[2,512,512]{2,1,0:T(8,128)(2,1)} %n_out.5) | copy-start | bytes 3145732
  20.8 7.6 %collective-permute-start.5 = (bf16[128,640]{1,0:T(8,128)(2,1)S(1)}, bf16[128,640]{1,0:T(8,128)(2,1)S(1)}, u32[]{:S(2)}, u32[]{:S(2)}) collective-permute-start(bf16[128,640]{1,0:T(8,128)(2,1)S(1)} %get-tuple-element.42), channel_id=1, source_target_pairs={{0,15},{1,2},{2,1},{3,4},{4,3},{5,6},{6,5},{7,8},{8,7},{9,10},{10,... | collective-permute-start | bytes 491528 | tf_op jit(solution)/shard_map/ppermute | solution.py:325
  21.6 1.3 %collective-permute-start.3 = (bf16[128,512]{1,0:T(8,128)(2,1)S(1)}, bf16[128,512]{1,0:T(8,128)(2,1)S(1)}, u32[]{:S(2)}, u32[]{:S(2)}) collective-permute-start(bf16[128,512]{1,0:T(8,128)(2,1)S(1)} %get-tuple-element.40), channel_id=1, source_target_pairs={{0,1},{1,0},{2,3},{3,2},{4,5},{5,4},{6,7},{7,6},{8,9},{9,8},{10,11... | collective-permute-start | bytes 393224 | tf_op jit(solution)/shard_map/ppermute | solution.py:328
  23.2 7.7 %collective-permute-start.4 = (bf16[128,512]{1,0:T(8,128)(2,1)S(1)}, bf16[128,512]{1,0:T(8,128)(2,1)S(1)}, u32[]{:S(2)}, u32[]{:S(2)}) collective-permute-start(bf16[128,512]{1,0:T(8,128)(2,1)S(1)} %rim_message.1._), channel_id=1, source_target_pairs={{0,15},{1,2},{2,1},{3,4},{4,3},{5,6},{6,5},{7,8},{8,7},{9,10},{10,... | collective-permute-start | bytes 393224 | tf_op jit(solution)/shard_map/ppermute | solution.py:325
  30.0 1.4 %collective-permute-start.6 = (bf16[128,512]{1,0:T(8,128)(2,1)S(1)}, bf16[128,512]{1,0:T(8,128)(2,1)S(1)}, u32[]{:S(2)}, u32[]{:S(2)}) collective-permute-start(bf16[128,512]{1,0:T(8,128)(2,1)S(1)} %get-tuple-element.50), channel_id=1, source_target_pairs={{0,1},{1,0},{2,3},{3,2},{4,5},{5,4},{6,7},{7,6},{8,9},{9,8},{10,11... | collective-permute-start | bytes 393224 | tf_op jit(solution)/shard_map/ppermute | solution.py:328

commit v2 on v1

--- a/solution.py
+++ b/solution.py
@@ -183,13 +183,18 @@
     return [(s.astype(F32) + x).astype(BF16) for s, x in zip(states, second)]
 
 
-def prepare_kernel(nbr, state, gain, w_self, coupling, pre, mix):
+def prepare_kernel(nbr_ref, state, gain, w_self, coupling, pre, mix, nbr, sem):
+    read = pltpu.make_async_copy(nbr_ref, nbr, sem)
+    read.start()
     blocks, rows = state.shape[0], state.shape[1]
     odd = odd_device()
     last = blocks + 1
     codes = [1 + c for c in range(blocks)] + [last * odd, last - last * odd]
+    normed = [norm_rows(state[m].astype(F32), gain[...]) for m in range(blocks)]
     for m in range(blocks):
-        pre[m] = dot(norm_rows(state[m].astype(F32), gain[...]), w_self[...])
+        pre[m] = dot(normed[m], w_self[...])
+    read.wait()
+    for m in range(blocks):
         before, after, other = [coupling[m, k] for k in range(1, 4)]
         zero = jnp.zeros_like(other)
         for c, code in enumerate(codes):
@@ -287,10 +292,11 @@
     rims = jnp.concatenate([far[...], on[...]], axis=0)
     each = range(blocks)
     incoming = [(message[m] + dot(mix[m, :, size:], rims)).astype(BF16) for m in each]
-    updated = updates([state[m] for m in each], [pre[m] for m in each], incoming, n_msg[1], n_out[1])
+    first = [dot(x, n_msg[1]) for x in incoming]
+    hidden = [silu(pre[m] + first[m]).astype(BF16) for m in each]
     copies = [pltpu.make_async_copy(stage.at[m], out.at[m], sems.at[m]) for m in each]
     for m in each:
-        stage[m] = updated[m]
+        stage[m] = (state[m].astype(F32) + dot(hidden[m], n_out[1])).astype(BF16)
         copies[m].start()
     for copy in copies:
         copy.wait()
@@ -346,7 +352,8 @@
         [shape(*whole, dtype=F32), shape(blocks, rows, size + 2 * rows)],
         [mesh_state, enc_gain[None], enc_self, mesh_coupling],
         "prepare",
-        scalars=[neighbor],
+        late=[neighbor],
+        scratch=(pltpu.SMEM(neighbor.shape, jnp.int32), pltpu.SemaphoreType.DMA),
         weight=34,
     )
     encode = [pre, mesh_state, sums_own, sums_on]

time: 33 us -> 33.1 us (level)
  Pallas kernels: 17.3 us -> 15.3 us
  waiting for transfers between devices: 2.23 us -> 4.12 us
  starting transfers between devices: 12.5 us -> 13.1 us
    pallas_call x3, Pallas kernels: 8.62 us -> 7 us  [pair_sums(): pl.pallas_call(kernel, input_output_aliases={5: 0} if late_only else {},...]
    ppermute x4, waiting for transfers between devices: 1.52 us -> 2.96 us  [swap_off(): return lax.ppermute(x, 'mesh', off_route)]
    ppermute x4, starting transfers between devices: 12.4 us -> 13 us  [swap_off(): return lax.ppermute(x, 'mesh', off_route)]
    ppermute x3, waiting for transfers between devices: 0.7 us -> 1.16 us  [swap_on(): return lax.ppermute(x, 'mesh', on_route)]
    pallas_call x11, Pallas kernels: 8.72 us -> 8.27 us  [call(): pl.pallas_call(kernel, out_shape=out, in_specs=[SMEM] * len(scalars) + [p...]
  transfers between devices with their start and end apart: 7 -> 7, of which waited for: 3 -> 4; matrix products, arithmetic and copies ran while one was open for 0% -> 0% of each run, Pallas kernels for 35% -> 30%
where the time goes in v2:
time: 33.1 us; the launch traced here: 33.5 us
  Pallas kernels  15.3 us (46%)
  starting transfers between devices  13.1 us (40%)
  waiting for transfers between devices  4.12 us (12%)
  between operations  0.96 us (3%)
    ppermute x4, starting transfers between devices, swap_off(): return lax.ppermute(x, 'mesh', off_route)  13 us
    pallas_call x11, Pallas kernels, call(): pl.pallas_call(kernel, out_shape=out, in_specs=[SMEM] * len(scalars) + [p...  8.27 us
    pallas_call x3, Pallas kernels, pair_sums(): pl.pallas_call(kernel, input_output_aliases={5: 0} if late_only else {},...  7 us
    ppermute x4, waiting for transfers between devices, swap_off(): return lax.ppermute(x, 'mesh', off_route)  2.96 us
    ppermute x3, waiting for transfers between devices, swap_on(): return lax.ppermute(x, 'mesh', on_route)  1.16 us
  transfers between devices with their start and end apart: 7, of which 4 were waited for; matrix products, arithmetic and copies ran while one was open for 0% of the time, Pallas kernels for 30%

profile of v2, /device:TPU:0, one launch (start us, length us, event | category | flops | bytes accessed | tf_op | source)
XLA Modules:
  0.0 33.5 jit_solution(17922418686841582611)
XLA Ops:
  0.7 2.9 %pairs_off_off.1 = (bf16[2,128,512]{2,1,0:T(8,128)(2,1)S(1)}, bf16[2,128,512]{2,1,0:T(8,128)(2,1)S(1)}) custom-call(s32[1]{0:T(128)S(6)} %copy.20.refs_0_, s32[32]{0:T(128)} %refs_1_.6, s32[32]{0:T(128)} %refs_2_.7, bf16[32,128,512]{2,1,0:T(8,128)(2,1)} %refs_3_.5, bf16[32,128,128]{2,1,0:T(8,128)(2,1)} %refs_4_.5), custom_call_target="tpu_custom_call" | custom-call | flops 1048576 | bytes 1048576 | tf_op jit(solution)/shard_map/pairs_off_off/pallas_call | solution.py:128
  3.6 5.6 %collective-permute-start.2 = (bf16[2,128,512]{2,1,0:T(8,128)(2,1)S(1)}, bf16[2,128,512]{2,1,0:T(8,128)(2,1)S(1)}, u32[]{:S(2)}, u32[]{:S(2)}) collective-permute-start(bf16[2,128,512]{2,1,0:T(8,128)(2,1)S(1)} %get-tuple-element.32.refs_6_), channel_id=1, source_target_pairs={{0,15},{1,2},{2,1},{3,4},{4,3},{5,6},{6,5},{7,8},{8,7},{9,10},{10,... | collective-permute-start | bytes 786440 | tf_op jit(solution)/shard_map/ppermute | solution.py:331
  9.1 0.3 pairs_off_late.1.refs_5_
  9.5 0.0 copy-start.3
  9.5 0.0 copy-start.10
  9.5 0.0 copy-start.11
  9.5 2.2 %collective-permute-start.1 = (bf16[2,128,512]{2,1,0:T(8,128)(2,1)S(1)}, bf16[2,128,512]{2,1,0:T(8,128)(2,1)S(1)}, u32[]{:S(2)}, u32[]{:S(2)}) collective-permute-start(bf16[2,128,512]{2,1,0:T(8,128)(2,1)S(1)} %pairs_off_late.1.refs_5_), channel_id=1, source_target_pairs={{0,15},{1,2},{2,1},{3,4},{4,3},{5,6},{6,5},{7,8},{8,7},{9,10},{10,... | collective-permute-start | bytes 786440 | tf_op jit(solution)/shard_map/ppermute | solution.py:331
  11.7 3.8 %pairs_on_self.1 = (bf16[4,128,512]{2,1,0:T(8,128)(2,1)S(1)}, f32[4,128,512]{2,1,0:T(8,128)S(1)}) custom-call(s32[1]{0:T(128)S(6)} %copy.20.refs_0_, s32[32]{0:T(128)} %refs_1_.6, s32[32]{0:T(128)} %refs_2_.7, bf16[32,128,512]{2,1,0:T(8,128)(2,1)} %refs_3_.5, bf16[32,128,128]{2,1,0:T(8,128)(2,1)} %refs_4_.5, bf16[2,128,512]{2,1,0:T(8,128)(2,1)S(1)} %pairs_off_late.1.refs_5_), custom_call_target="tpu_custom_call" | custom-call | flops 1048576 | bytes 1048576 | tf_op jit(solution)/shard_map/pairs_on_self/pallas_call | solution.py:128
  15.5 0.1 collective-permute-start
  15.7 0.0 copy-start.6
  15.7 1.0 %prepare.1 = (f32[4,128,512]{2,1,0:T(8,128)S(1)}, bf16[4,128,768]{2,1,0:T(8,128)(2,1)S(1)}) custom-call(s32[4,4]{1,0:T(4,128)S(1)} %copy-done.10, bf16[4,128,512]{2,1,0:T(8,128)(2,1)S(1)} %copy-done.3, f32[1,512]{1,0:T(1,128)S(1)} %bitcast.1, bf16[512,512]{1,0:T(8,128)(2,1)S(1)} %copy-done.8, bf16[4,4,128,128]{3,2,1,0:T(8,128)(2,1)S(1)} %copy-done.9), custom_call_target="tpu_custom_call" | custom-call | flops 17179869184 | bytes 1048576 | tf_op jit(solution)/shard_map/prepare/pallas_call | solution.py:152
  16.7 0.0 copy-start.7
  16.7 0.8 %collective-permute-done.refs_3_.on = bf16[4,128,512]{2,1,0:T(8,128)(2,1)S(1)} collective-permute-done((bf16[4,128,512]{2,1,0:T(8,128)(2,1)S(1)}, bf16[4,128,512]{2,1,0:T(8,128)(2,1)S(1)}, u32[]{:S(2)}, u32[]{:S(2)}) %collective-permute-start) | collective-permute-done | bytes 524320 | tf_op jit(solution)/shard_map/ppermute | solution.py:334
  17.5 0.7 %encode_first.1 = (bf16[2,128,512]{2,1,0:T(8,128)(2,1)S(1)}, bf16[2,128,512]{2,1,0:T(8,128)(2,1)S(1)}) custom-call(f32[4,128,512]{2,1,0:T(8,128)S(1)} %get-tuple-element.30.refs_0_.pre, bf16[4,128,512]{2,1,0:T(8,128)(2,1)S(1)} %copy-done.3, f32[4,128,512]{2,1,0:T(8,128)S(1)} %get-tuple-element.33.refs_2_.own, ...), custom_call_target="tpu_custom_call" | custom-call | flops 1048576 | bytes 1048576 | tf_op jit(solution)/shard_map/encode_first/pallas_call | solution.py:152
  18.2 0.0 copy-start
  18.2 0.8 %encode_rest.1 = (bf16[4,128,512]{2,1,0:T(8,128)(2,1)S(1)}, bf16[4,128,512]{2,1,0:T(8,128)(2,1)S(1)}, bf16[128,512]{1,0:T(8,128)(2,1)S(1)}, bf16[128,512]{1,0:T(...) custom-call(s32[1,2]{1,0:T(1,128)S(1)} %copy-done.7, ...), custom_call_target="tpu_custom_call" | custom-call | flops 1048576 | bytes 1048576 | tf_op jit(solution)/shard_map/encode_rest/pallas_call | solution.py:152
  19.1 0.0 copy-start.1
  19.1 0.0 copy-start.2
  19.1 3.5 %collective-permute-start.5 = (bf16[128,640]{1,0:T(8,128)(2,1)S(1)}, bf16[128,640]{1,0:T(8,128)(2,1)S(1)}, u32[]{:S(2)}, u32[]{:S(2)}) collective-permute-start(bf16[128,640]{1,0:T(8,128)(2,1)S(1)} %get-tuple-element.42), channel_id=1, source_target_pairs={{0,15},{1,2},{2,1},{3,4},{4,3},{5,6},{6,5},{7,8},{8,7},{9,10},{10,... | collective-permute-start | bytes 491528 | tf_op jit(solution)/shard_map/ppermute | solution.py:331
  22.6 0.2 rim_part.1.part
  22.8 0.7 %round_0_local.1 = (f32[4,128,512]{2,1,0:T(8,128)S(1)}, f32[4,128,512]{2,1,0:T(8,128)S(1)}) custom-call(bf16[4,128,768]{2,1,0:T(8,128)(2,1)S(1)} %get-tuple-element.37.mix.refs_0_, bf16[4,128,512]{2,1,0:T(8,128)(2,1)S(1)} %get-tuple-element.39.normed.refs_1_, bf16[2,512,512]{2,1,0:T(8,128)(2,1)S(1)} %copy-done), custom_call_target="tpu_custom_call" | custom-call | flops 1048576 | bytes 1048576 | tf_op jit(solution)/shard_map/round_0_local/pallas_call | solution.py:152
  23.5 0.4 %collective-permute-done.3.on = bf16[128,512]{1,0:T(8,128)(2,1)S(1)} collective-permute-done((bf16[128,512]{1,0:T(8,128)(2,1)S(1)}, bf16[128,512]{1,0:T(8,128)(2,1)S(1)}, u32[]{:S(2)}, u32[]{:S(2)}) %collective-permute-start.3) | collective-permute-done | bytes 131104 | tf_op jit(solution)/shard_map/ppermute | solution.py:334
  23.9 0.2 rim_message.1._
  24.1 1.7 %collective-permute-start.4 = (bf16[128,512]{1,0:T(8,128)(2,1)S(1)}, bf16[128,512]{1,0:T(8,128)(2,1)S(1)}, u32[]{:S(2)}, u32[]{:S(2)}) collective-permute-start(bf16[128,512]{1,0:T(8,128)(2,1)S(1)} %rim_message.1._), channel_id=1, source_target_pairs={{0,15},{1,2},{2,1},{3,4},{4,3},{5,6},{6,5},{7,8},{8,7},{9,10},{10,... | collective-permute-start | bytes 393224 | tf_op jit(solution)/shard_map/ppermute | solution.py:331
  25.8 0.8 %collective-permute-done.5.packed = bf16[128,640]{1,0:T(8,128)(2,1)S(1)} collective-permute-done((bf16[128,640]{1,0:T(8,128)(2,1)S(1)}, bf16[128,640]{1,0:T(8,128)(2,1)S(1)}, u32[]{:S(2)}, u32[]{:S(2)}) %collective-permute-start.5) | collective-permute-done | bytes 163872 | tf_op jit(solution)/shard_map/ppermute | solution.py:331
  26.6 0.4 %neighbour_rim.1 = (bf16[128,512]{1,0:T(8,128)(2,1)S(1)}, bf16[128,512]{1,0:T(8,128)(2,1)S(1)}, f32[128,512]{1,0:T(8,128)S(1)}, f32[128,512]{1,0:T(8,128)S(1)}) custom-call(bf16[128,640]{1,0:T(8,128)(2,1)S(1)} %collective-permute-done.5.packed, bf16[128,512]{1,0:T(8,128)(2,1)S(1)} %get-tuple-element.43.rim_off, f32[2,512]{1,0:T(2,128)S(1)} %copy-done.6, ...), custom_call_target="tpu_custom_call" | custom-call | flops 1048576 | bytes 1048576 | tf_op jit(solution)/shard_map/neighbour_rim/pallas_call | solution.py:152
  27.0 1.2 %round_0.1 = (bf16[4,128,512]{2,1,0:T(8,128)(2,1)S(1)}, bf16[4,128,512]{2,1,0:T(8,128)(2,1)S(1)}, bf16[128,512]{1,0:T(8,128)(2,1)S(1)}) custom-call(s32[1,2]{1,0:T(1,128)S(1)} %copy-done.7, bf16[4,128,768]{2,1,0:T(8,128)(2,1)S(1)} %get-tuple-element.37.mix.refs_0_, bf16[128,512]{1,0:T(8,128)(2,1)S(1)} %get-tuple-element.47.off, ...), custom_call_target="tpu_custom_call" | custom-call | flops 1048576 | bytes 1048576 | tf_op jit(solution)/shard_map/round_0/pallas_call | solution.py:152
  28.3 0.1 collective-permute-start.6
  28.4 0.7 %round_1_local.1 = (f32[4,128,512]{2,1,0:T(8,128)S(1)}, f32[4,128,512]{2,1,0:T(8,128)S(1)}) custom-call(bf16[4,128,768]{2,1,0:T(8,128)(2,1)S(1)} %get-tuple-element.37.mix.refs_0_, bf16[4,128,512]{2,1,0:T(8,128)(2,1)S(1)} %get-tuple-element.51.refs_1_, bf16[2,512,512]{2,1,0:T(8,128)(2,1)S(1)} %copy-done), custom_call_target="tpu_custom_call" | custom-call | flops 1048576 | bytes 1048576 | tf_op jit(solution)/shard_map/round_1_local/pallas_call | solution.py:152
  29.1 2.2 %collective-permute-done.4.arrived = bf16[128,512]{1,0:T(8,128)(2,1)S(1)} collective-permute-done((bf16[128,512]{1,0:T(8,128)(2,1)S(1)}, bf16[128,512]{1,0:T(8,128)(2,1)S(1)}, u32[]{:S(2)}, u32[]{:S(2)}) %collective-permute-start.4) | collective-permute-done | bytes 131104 | tf_op jit(solution)/shard_map/ppermute | solution.py:331
  31.3 0.6 %far_rim.1.far = bf16[128,512]{1,0:T(8,128)(2,1)S(1)} custom-call(bf16[128,512]{1,0:T(8,128)(2,1)S(1)} %collective-permute-done.4.arrived, f32[128,512]{1,0:T(8,128)S(1)} %get-tuple-element.44.far_message, f32[128,512]{1,0:T(8,128)S(1)} %get-tuple-element.45.pre, bf16[128,512]{1,0:T(8,128)(2,1)S(1)} %get-tuple-element.46.state, ...), custom_call_target="tpu_custom_call" | custom-call | flops 1048576 | bytes 1048576 | tf_op jit(solution)/shard_map/far_rim/pallas_call | solution.py:152
  31.9 1.6 %round_1.1 = bf16[4,128,512]{2,1,0:T(8,128)(2,1)} custom-call(bf16[128,512]{1,0:T(8,128)(2,1)S(1)} %far_rim.1.far, bf16[128,512]{1,0:T(8,128)(2,1)S(1)} %collective-permute-done.6.on, bf16[4,128,768]{2,1,0:T(8,128)(2,1)S(1)} %get-tuple-element.37.mix.refs_0_, f32[4,128,512]{2,1,0:T(8,128)S(1)} %get-tuple-element.52.pre, ...), custom_call_target="tpu_custom_call" | custom-call | flops 1048576 | bytes 1048576 | tf_op jit(solution)/shard_map/round_1/pallas_call | solution.py:152
  (20 shorter events, 0.1 us)
Async XLA Ops:
  3.6 13.1 %collective-permute-start.2 = (bf16[2,128,512]{2,1,0:T(8,128)(2,1)S(1)}, bf16[2,128,512]{2,1,0:T(8,128)(2,1)S(1)}, u32[]{:S(2)}, u32[]{:S(2)}) collective-permute-start(bf16[2,128,512]{2,1,0:T(8,128)(2,1)S(1)} %get-tuple-element.32.refs_6_), channel_id=1, source_target_pairs={{0,15},{1,2},{2,1},{3,4},{4,3},{5,6},{6,5},{7,8},{8,7},{9,10},{10,... | collective-permute-start | bytes 786440 | tf_op jit(solution)/shard_map/ppermute | solution.py:331
  9.5 6.1 %copy-start.3 = (bf16[4,128,512]{2,1,0:T(8,128)(2,1)S(1)}, bf16[4,128,512]{2,1,0:T(8,128)(2,1)}, u32[]{:S(2)}) copy-start(bf16[4,128,512]{2,1,0:T(8,128)(2,1)} %base.1) | copy-start | bytes 1572868
  9.5 6.1 %copy-start.8 = (bf16[512,512]{1,0:T(8,128)(2,1)S(1)}, bf16[512,512]{1,0:T(8,128)(2,1)}, u32[]{:S(2)}) copy-start(bf16[512,512]{1,0:T(8,128)(2,1)} %w_self.1) | copy-start | bytes 1572868
  9.5 6.1 %copy-start.9 = (bf16[4,4,128,128]{3,2,1,0:T(8,128)(2,1)S(1)}, bf16[4,4,128,128]{3,2,1,0:T(8,128)(2,1)}, u32[]{:S(2)}) copy-start(bf16[4,4,128,128]{3,2,1,0:T(8,128)(2,1)} %coupling.1) | copy-start | bytes 1572868
  9.5 6.1 %copy-start.10 = (s32[4,4]{1,0:T(4,128)S(1)}, s32[4,4]{1,0:T(4,128)}, u32[]{:S(2)}) copy-start(s32[4,4]{1,0:T(4,128)} %nbr_ref.1) | copy-start | bytes 196
  9.5 6.1 %copy-start.11 = (f32[512]{0:T(512)S(1)}, f32[512]{0:T(512)}, u32[]{:S(2)}) copy-start(f32[512]{0:T(512)} %param.26) | copy-start | bytes 6148
  9.5 8.7 %collective-permute-start.1 = (bf16[2,128,512]{2,1,0:T(8,128)(2,1)S(1)}, bf16[2,128,512]{2,1,0:T(8,128)(2,1)S(1)}, u32[]{:S(2)}, u32[]{:S(2)}) collective-permute-start(bf16[2,128,512]{2,1,0:T(8,128)(2,1)S(1)} %pairs_off_late.1.refs_5_), channel_id=1, source_target_pairs={{0,15},{1,2},{2,1},{3,4},{4,3},{5,6},{6,5},{7,8},{8,7},{9,10},{10,... | collective-permute-start | bytes 786440 | tf_op jit(solution)/shard_map/ppermute | solution.py:331
  15.5 2.0 %collective-permute-start = (bf16[4,128,512]{2,1,0:T(8,128)(2,1)S(1)}, bf16[4,128,512]{2,1,0:T(8,128)(2,1)S(1)}, u32[]{:S(2)}, u32[]{:S(2)}) collective-permute-start(bf16[4,128,512]{2,1,0:T(8,128)(2,1)S(1)} %get-tuple-element.34), channel_id=1, source_target_pairs={{0,1},{1,0},{2,3},{3,2},{4,5},{5,4},{6,7},{7,6},{8,9},{9,8},{10,11... | collective-permute-start | bytes 1572872 | tf_op jit(solution)/shard_map/ppermute | solution.py:334
  15.6 1.8 %copy-start.4 = (bf16[512,512]{1,0:T(8,128)(2,1)S(1)}, bf16[512,512]{1,0:T(8,128)(2,1)}, u32[]{:S(2)}) copy-start(bf16[512,512]{1,0:T(8,128)(2,1)} %w_obs.1) | copy-start | bytes 1572868
  15.6 1.8 %copy-start.5 = (bf16[512,512]{1,0:T(8,128)(2,1)S(1)}, bf16[512,512]{1,0:T(8,128)(2,1)}, u32[]{:S(2)}) copy-start(bf16[512,512]{1,0:T(8,128)(2,1)} %w_out.1) | copy-start | bytes 1572868
  15.7 1.8 %copy-start.6 = (f32[2,512]{1,0:T(2,128)S(1)}, f32[2,512]{1,0:T(2,128)}, u32[]{:S(2)}) copy-start(f32[2,512]{1,0:T(2,128)} %gain.5) | copy-start | bytes 12292
  16.7 1.6 %copy-start.7 = (s32[1,2]{1,0:T(1,128)S(1)}, s32[1,2]{1,0:T(1,128)}, u32[]{:S(2)}) copy-start(s32[1,2]{1,0:T(1,128)} %rim_ref.3) | copy-start | bytes 28
  18.2 4.6 %copy-start = (bf16[2,512,512]{2,1,0:T(8,128)(2,1)S(1)}, bf16[2,512,512]{2,1,0:T(8,128)(2,1)}, u32[]{:S(2)}) copy-start(bf16[2,512,512]{2,1,0:T(8,128)(2,1)} %refs_2_.9) | copy-start | bytes 3145732
  19.1 8.0 %copy-start.1 = (bf16[2,512,512]{2,1,0:T(8,128)(2,1)S(1)}, bf16[2,512,512]{2,1,0:T(8,128)(2,1)}, u32[]{:S(2)}) copy-start(bf16[2,512,512]{2,1,0:T(8,128)(2,1)} %n_msg.5) | copy-start | bytes 3145732
  19.1 8.0 %copy-start.2 = (bf16[2,512,512]{2,1,0:T(8,128)(2,1)S(1)}, bf16[2,512,512]{2,1,0:T(8,128)(2,1)}, u32[]{:S(2)}) copy-start(bf16[2,512,512]{2,1,0:T(8,128)(2,1)} %n_out.5) | copy-start | bytes 3145732
  19.1 7.5 %collective-permute-start.5 = (bf16[128,640]{1,0:T(8,128)(2,1)S(1)}, bf16[128,640]{1,0:T(8,128)(2,1)S(1)}, u32[]{:S(2)}, u32[]{:S(2)}) collective-permute-start(bf16[128,640]{1,0:T(8,128)(2,1)S(1)} %get-tuple-element.42), channel_id=1, source_target_pairs={{0,15},{1,2},{2,1},{3,4},{4,3},{5,6},{6,5},{7,8},{8,7},{9,10},{10,... | collective-permute-start | bytes 491528 | tf_op jit(solution)/shard_map/ppermute | solution.py:331
  22.6 1.3 %collective-permute-start.3 = (bf16[128,512]{1,0:T(8,128)(2,1)S(1)}, bf16[128,512]{1,0:T(8,128)(2,1)S(1)}, u32[]{:S(2)}, u32[]{:S(2)}) collective-permute-start(bf16[128,512]{1,0:T(8,128)(2,1)S(1)} %get-tuple-element.40), channel_id=1, source_target_pairs={{0,1},{1,0},{2,3},{3,2},{4,5},{5,4},{6,7},{7,6},{8,9},{9,8},{10,11... | collective-permute-start | bytes 393224 | tf_op jit(solution)/shard_map/ppermute | solution.py:334
  24.1 7.2 %collective-permute-start.4 = (bf16[128,512]{1,0:T(8,128)(2,1)S(1)}, bf16[128,512]{1,0:T(8,128)(2,1)S(1)}, u32[]{:S(2)}, u32[]{:S(2)}) collective-permute-start(bf16[128,512]{1,0:T(8,128)(2,1)S(1)} %rim_message.1._), channel_id=1, source_target_pairs={{0,15},{1,2},{2,1},{3,4},{4,3},{5,6},{6,5},{7,8},{8,7},{9,10},{10,... | collective-permute-start | bytes 393224 | tf_op jit(solution)/shard_map/ppermute | solution.py:331
  28.3 3.6 %collective-permute-start.6 = (bf16[128,512]{1,0:T(8,128)(2,1)S(1)}, bf16[128,512]{1,0:T(8,128)(2,1)S(1)}, u32[]{:S(2)}, u32[]{:S(2)}) collective-permute-start(bf16[128,512]{1,0:T(8,128)(2,1)S(1)} %get-tuple-element.50), channel_id=1, source_target_pairs={{0,1},{1,0},{2,3},{3,2},{4,5},{5,4},{6,7},{7,6},{8,9},{9,8},{10,11... | collective-permute-start | bytes 393224 | tf_op jit(solution)/shard_map/ppermute | solution.py:334

commit v3 on v1

--- a/solution.py
+++ b/solution.py
@@ -243,14 +243,15 @@
     message[...] = (part[...] + dot(row[:, row.shape[1] - on.shape[0] :], on[...])).astype(BF16)
 
 
-def neighbour_kernel(packed, rim_off, node_gain, n_self, _, state, normed, pre, message):
-    rows, width = state.shape
-    values = packed[:, :width]
+def neighbour_kernel(packed, node_gain, _, state, normed):
+    values = packed[:, : state.shape[1]]
     state[...] = values
-    result = norm_rows(values.astype(F32), node_gain[:1, :])
-    normed[...] = result
-    pre[...] = dot(result, n_self[0])
-    message[...] = dot(packed[:, width:], rim_off[...])
+    normed[...] = norm_rows(values.astype(F32), node_gain[:1, :])
+
+
+def far_part_kernel(packed, rim_off, far, n_self, _, pre, message):
+    pre[...] = dot(far[...], n_self[0])
+    message[...] = dot(packed[:, far.shape[1] :], rim_off[...])
 
 
 def round_kernel(rim_ref, mix, off, on, pre, heard, state, n_msg, n_out, gain, new_state, new_normed, rim_on, rim, sem):
@@ -381,10 +382,10 @@
     )
     (message,) = call(message_kernel, [shape(*block)], [row, part, on, heard], "rim_message")
     arrived = swap_off(message)
-    far_state, far, far_pre, far_message = call(
+    far_state, far = call(
         neighbour_kernel,
-        [shape(*block), shape(*block), shape(*block, dtype=F32), shape(*block, dtype=F32)],
-        [packed, rim_off, node_gain, node_self, message],
+        [shape(*block), shape(*block)],
+        [packed, node_gain, message],
         "neighbour_rim",
     )
     state, normed, rim_on = call(
@@ -401,6 +402,12 @@
         [shape(*whole, dtype=F32), shape(*whole, dtype=F32)],
         [mix, normed, node_self],
         "round_1_local",
+    )
+    far_pre, far_message = call(
+        far_part_kernel,
+        [shape(*block, dtype=F32), shape(*block, dtype=F32)],
+        [packed, rim_off, far, node_self, rim_on],
+        "far_part",
     )
     (far,) = call(
         far_kernel,

time: 33 us -> 32.6 us (0.988)
  Pallas kernels: 17.3 us -> 15.2 us
  waiting for transfers between devices: 2.23 us -> 3.69 us
    pallas_call x3, Pallas kernels: 8.62 us -> 6.48 us  [pair_sums(): pl.pallas_call(kernel, input_output_aliases={5: 0} if late_only else {},...]
    ppermute x4, waiting for transfers between devices: 1.52 us -> 2.99 us  [swap_off(): return lax.ppermute(x, 'mesh', off_route)]
    pallas_call x11 -> x12, Pallas kernels: 8.72 us -> 8.76 us  [call(): pl.pallas_call(kernel, out_shape=out, in_specs=[SMEM] * len(scalars) + [p...]
  transfers between devices with their start and end apart: 7 -> 7, of which waited for: 3 -> 5; matrix products, arithmetic and copies ran while one was open for 0% -> 0% of each run, Pallas kernels for 35% -> 31%
where the time goes in v3:
time: 32.6 us
  Pallas kernels  15.2 us (47%)
  starting transfers between devices  12.7 us (39%)
  waiting for transfers between devices  3.69 us (11%)
  between operations  0.93 us (3%)
    ppermute x4, starting transfers between devices, swap_off(): return lax.ppermute(x, 'mesh', off_route)  12.5 us
    pallas_call x12, Pallas kernels, call(): pl.pallas_call(kernel, out_shape=out, in_specs=[SMEM] * len(scalars) + [p...  8.76 us
    pallas_call x3, Pallas kernels, pair_sums(): pl.pallas_call(kernel, input_output_aliases={5: 0} if late_only else {},...  6.48 us
    ppermute x4, waiting for transfers between devices, swap_off(): return lax.ppermute(x, 'mesh', off_route)  2.99 us
    ppermute x3, waiting for transfers between devices, swap_on(): return lax.ppermute(x, 'mesh', on_route)  0.71 us
  transfers between devices with their start and end apart: 7, of which 5 were waited for; matrix products, arithmetic and copies ran while one was open for 0% of the time, Pallas kernels for 31%

profile of v3, /device:TPU:0, one launch (start us, length us, event | category | flops | bytes accessed | tf_op | source)
XLA Modules:
  0.0 32.6 jit_solution(4049076451341598095)
XLA Ops:
  0.7 2.8 %pairs_off_off.1 = (bf16[2,128,512]{2,1,0:T(8,128)(2,1)S(1)}, bf16[2,128,512]{2,1,0:T(8,128)(2,1)S(1)}) custom-call(s32[1]{0:T(128)S(6)} %copy.20.refs_0_, s32[32]{0:T(128)} %refs_1_.6, s32[32]{0:T(128)} %refs_2_.7, bf16[32,128,512]{2,1,0:T(8,128)(2,1)} %refs_3_.5, bf16[32,128,128]{2,1,0:T(8,128)(2,1)} %refs_4_.5), custom_call_target="tpu_custom_call" | custom-call | flops 1048576 | bytes 1048576 | tf_op jit(solution)/shard_map/pairs_off_off/pallas_call | solution.py:128
  3.5 5.5 %collective-permute-start.2 = (bf16[2,128,512]{2,1,0:T(8,128)(2,1)S(1)}, bf16[2,128,512]{2,1,0:T(8,128)(2,1)S(1)}, u32[]{:S(2)}, u32[]{:S(2)}) collective-permute-start(bf16[2,128,512]{2,1,0:T(8,128)(2,1)S(1)} %get-tuple-element.32.refs_6_), channel_id=1, source_target_pairs={{0,15},{1,2},{2,1},{3,4},{4,3},{5,6},{6,5},{7,8},{8,7},{9,10},{10,... | collective-permute-start | bytes 786440 | tf_op jit(solution)/shard_map/ppermute | solution.py:326
  9.0 0.3 pairs_off_late.1.refs_5_
  9.3 0.0 copy-start.3
  9.4 0.0 copy-start.9
  9.4 0.0 copy-start.10
  9.4 2.1 %collective-permute-start.1 = (bf16[2,128,512]{2,1,0:T(8,128)(2,1)S(1)}, bf16[2,128,512]{2,1,0:T(8,128)(2,1)S(1)}, u32[]{:S(2)}, u32[]{:S(2)}) collective-permute-start(bf16[2,128,512]{2,1,0:T(8,128)(2,1)S(1)} %pairs_off_late.1.refs_5_), channel_id=1, source_target_pairs={{0,15},{1,2},{2,1},{3,4},{4,3},{5,6},{6,5},{7,8},{8,7},{9,10},{10,... | collective-permute-start | bytes 786440 | tf_op jit(solution)/shard_map/ppermute | solution.py:326
  11.5 3.3 %pairs_on_self.1 = (bf16[4,128,512]{2,1,0:T(8,128)(2,1)S(1)}, f32[4,128,512]{2,1,0:T(8,128)S(1)}) custom-call(s32[1]{0:T(128)S(6)} %copy.20.refs_0_, s32[32]{0:T(128)} %refs_1_.6, s32[32]{0:T(128)} %refs_2_.7, bf16[32,128,512]{2,1,0:T(8,128)(2,1)} %refs_3_.5, bf16[32,128,128]{2,1,0:T(8,128)(2,1)} %refs_4_.5, bf16[2,128,512]{2,1,0:T(8,128)(2,1)S(1)} %pairs_off_late.1.refs_5_), custom_call_target="tpu_custom_call" | custom-call | flops 1048576 | bytes 1048576 | tf_op jit(solution)/shard_map/pairs_on_self/pallas_call | solution.py:128
  14.9 0.1 collective-permute-start
  15.0 0.0 copy-start.4
  15.0 0.0 copy-start.5
  15.0 1.5 %prepare.1 = (f32[4,128,512]{2,1,0:T(8,128)S(1)}, bf16[4,128,768]{2,1,0:T(8,128)(2,1)S(1)}) custom-call(s32[4,4]{1,0:T(4,128)S(1)} %copy-done.10, bf16[4,128,512]{2,1,0:T(8,128)(2,1)S(1)} %copy-done.3, f32[1,512]{1,0:T(1,128)S(1)} %bitcast.1, bf16[512,512]{1,0:T(8,128)(2,1)S(1)} %copy-done.8, bf16[4,4,128,128]{3,2,1,0:T(8,128)(2,1)S(1)} %copy-done.9), custom_call_target="tpu_custom_call" | custom-call | flops 17179869184 | bytes 1048576 | tf_op jit(solution)/shard_map/prepare/pallas_call | solution.py:152
  16.5 0.3 collective-permute-done.refs_3_.on
  16.8 0.7 %encode_first.1 = (bf16[2,128,512]{2,1,0:T(8,128)(2,1)S(1)}, bf16[2,128,512]{2,1,0:T(8,128)(2,1)S(1)}) custom-call(f32[4,128,512]{2,1,0:T(8,128)S(1)} %get-tuple-element.30.refs_0_.pre, bf16[4,128,512]{2,1,0:T(8,128)(2,1)S(1)} %copy-done.3, f32[4,128,512]{2,1,0:T(8,128)S(1)} %get-tuple-element.33.refs_2_.own, ...), custom_call_target="tpu_custom_call" | custom-call | flops 1048576 | bytes 1048576 | tf_op jit(solution)/shard_map/encode_first/pallas_call | solution.py:152
  17.6 0.0 copy-start
  17.6 0.5 %collective-permute-done.1.off = bf16[2,128,512]{2,1,0:T(8,128)(2,1)S(1)} collective-permute-done((bf16[2,128,512]{2,1,0:T(8,128)(2,1)S(1)}, bf16[2,128,512]{2,1,0:T(8,128)(2,1)S(1)}, u32[]{:S(2)}, u32[]{:S(2)}) %collective-permute-start.1) | collective-permute-done | bytes 262176 | tf_op jit(solution)/shard_map/ppermute | solution.py:326
  18.1 0.8 %encode_rest.1 = (bf16[4,128,512]{2,1,0:T(8,128)(2,1)S(1)}, bf16[4,128,512]{2,1,0:T(8,128)(2,1)S(1)}, bf16[128,512]{1,0:T(8,128)(2,1)S(1)}, bf16[128,512]{1,0:T(...) custom-call(s32[1,2]{1,0:T(1,128)S(1)} %copy-done.7, ...), custom_call_target="tpu_custom_call" | custom-call | flops 1048576 | bytes 1048576 | tf_op jit(solution)/shard_map/encode_rest/pallas_call | solution.py:152
  18.9 2.8 %collective-permute-start.5 = (bf16[128,640]{1,0:T(8,128)(2,1)S(1)}, bf16[128,640]{1,0:T(8,128)(2,1)S(1)}, u32[]{:S(2)}, u32[]{:S(2)}) collective-permute-start(bf16[128,640]{1,0:T(8,128)(2,1)S(1)} %get-tuple-element.42), channel_id=1, source_target_pairs={{0,15},{1,2},{2,1},{3,4},{4,3},{5,6},{6,5},{7,8},{8,7},{9,10},{10,... | collective-permute-start | bytes 491528 | tf_op jit(solution)/shard_map/ppermute | solution.py:326
  21.7 0.2 rim_part.1.part
  21.9 0.7 %round_0_local.1 = (f32[4,128,512]{2,1,0:T(8,128)S(1)}, f32[4,128,512]{2,1,0:T(8,128)S(1)}) custom-call(bf16[4,128,768]{2,1,0:T(8,128)(2,1)S(1)} %get-tuple-element.37.mix.refs_0_, bf16[4,128,512]{2,1,0:T(8,128)(2,1)S(1)} %get-tuple-element.39.normed.refs_1_, bf16[2,512,512]{2,1,0:T(8,128)(2,1)S(1)} %copy-done), custom_call_target="tpu_custom_call" | custom-call | flops 1048576 | bytes 1048576 | tf_op jit(solution)/shard_map/round_0_local/pallas_call | solution.py:152
  22.6 0.4 %collective-permute-done.3.on = bf16[128,512]{1,0:T(8,128)(2,1)S(1)} collective-permute-done((bf16[128,512]{1,0:T(8,128)(2,1)S(1)}, bf16[128,512]{1,0:T(8,128)(2,1)S(1)}, u32[]{:S(2)}, u32[]{:S(2)}) %collective-permute-start.3) | collective-permute-done | bytes 131104 | tf_op jit(solution)/shard_map/ppermute | solution.py:329
  23.0 0.2 rim_message.1._
  23.2 2.1 %collective-permute-start.4 = (bf16[128,512]{1,0:T(8,128)(2,1)S(1)}, bf16[128,512]{1,0:T(8,128)(2,1)S(1)}, u32[]{:S(2)}, u32[]{:S(2)}) collective-permute-start(bf16[128,512]{1,0:T(8,128)(2,1)S(1)} %rim_message.1._), channel_id=1, source_target_pairs={{0,15},{1,2},{2,1},{3,4},{4,3},{5,6},{6,5},{7,8},{8,7},{9,10},{10,... | collective-permute-start | bytes 393224 | tf_op jit(solution)/shard_map/ppermute | solution.py:326
  25.3 1.2 %collective-permute-done.5.packed = bf16[128,640]{1,0:T(8,128)(2,1)S(1)} collective-permute-done((bf16[128,640]{1,0:T(8,128)(2,1)S(1)}, bf16[128,640]{1,0:T(8,128)(2,1)S(1)}, u32[]{:S(2)}, u32[]{:S(2)}) %collective-permute-start.5) | collective-permute-done | bytes 163872 | tf_op jit(solution)/shard_map/ppermute | solution.py:326
  26.5 0.2 neighbour_rim.1
  26.7 1.2 %round_0.1 = (bf16[4,128,512]{2,1,0:T(8,128)(2,1)S(1)}, bf16[4,128,512]{2,1,0:T(8,128)(2,1)S(1)}, bf16[128,512]{1,0:T(8,128)(2,1)S(1)}) custom-call(s32[1,2]{1,0:T(1,128)S(1)} %copy-done.7, bf16[4,128,768]{2,1,0:T(8,128)(2,1)S(1)} %get-tuple-element.37.mix.refs_0_, bf16[128,512]{1,0:T(8,128)(2,1)S(1)} %get-tuple-element.44.off.far, ...), custom_call_target="tpu_custom_call" | custom-call | flops 1048576 | bytes 1048576 | tf_op jit(solution)/shard_map/round_0/pallas_call | solution.py:152
  28.0 0.1 collective-permute-start.6
  28.1 0.7 %round_1_local.1 = (f32[4,128,512]{2,1,0:T(8,128)S(1)}, f32[4,128,512]{2,1,0:T(8,128)S(1)}) custom-call(bf16[4,128,768]{2,1,0:T(8,128)(2,1)S(1)} %get-tuple-element.37.mix.refs_0_, bf16[4,128,512]{2,1,0:T(8,128)(2,1)S(1)} %get-tuple-element.51.refs_1_, bf16[2,512,512]{2,1,0:T(8,128)(2,1)S(1)} %copy-done), custom_call_target="tpu_custom_call" | custom-call | flops 1048576 | bytes 1048576 | tf_op jit(solution)/shard_map/round_1_local/pallas_call | solution.py:152
  28.8 0.3 far_part.1
  29.0 1.3 %collective-permute-done.4.arrived = bf16[128,512]{1,0:T(8,128)(2,1)S(1)} collective-permute-done((bf16[128,512]{1,0:T(8,128)(2,1)S(1)}, bf16[128,512]{1,0:T(8,128)(2,1)S(1)}, u32[]{:S(2)}, u32[]{:S(2)}) %collective-permute-start.4) | collective-permute-done | bytes 131104 | tf_op jit(solution)/shard_map/ppermute | solution.py:326
  30.4 0.6 %far_rim.1.far = bf16[128,512]{1,0:T(8,128)(2,1)S(1)} custom-call(bf16[128,512]{1,0:T(8,128)(2,1)S(1)} %collective-permute-done.4.arrived, f32[128,512]{1,0:T(8,128)S(1)} %get-tuple-element.48.far_message, f32[128,512]{1,0:T(8,128)S(1)} %get-tuple-element.49.pre, bf16[128,512]{1,0:T(8,128)(2,1)S(1)} %get-tuple-element.50.state, ...), custom_call_target="tpu_custom_call" | custom-call | flops 1048576 | bytes 1048576 | tf_op jit(solution)/shard_map/far_rim/pallas_call | solution.py:152
  31.0 1.6 %round_1.1 = bf16[4,128,512]{2,1,0:T(8,128)(2,1)} custom-call(bf16[128,512]{1,0:T(8,128)(2,1)S(1)} %far_rim.1.far, bf16[128,512]{1,0:T(8,128)(2,1)S(1)} %collective-permute-done.6.on, bf16[4,128,768]{2,1,0:T(8,128)(2,1)S(1)} %get-tuple-element.37.mix.refs_0_, f32[4,128,512]{2,1,0:T(8,128)S(1)} %get-tuple-element.52.pre, ...), custom_call_target="tpu_custom_call" | custom-call | flops 1048576 | bytes 1048576 | tf_op jit(solution)/shard_map/round_1/pallas_call | solution.py:152
  (21 shorter events, 0.1 us)
Async XLA Ops:
  3.5 13.0 %collective-permute-start.2 = (bf16[2,128,512]{2,1,0:T(8,128)(2,1)S(1)}, bf16[2,128,512]{2,1,0:T(8,128)(2,1)S(1)}, u32[]{:S(2)}, u32[]{:S(2)}) collective-permute-start(bf16[2,128,512]{2,1,0:T(8,128)(2,1)S(1)} %get-tuple-element.32.refs_6_), channel_id=1, source_target_pairs={{0,15},{1,2},{2,1},{3,4},{4,3},{5,6},{6,5},{7,8},{8,7},{9,10},{10,... | collective-permute-start | bytes 786440 | tf_op jit(solution)/shard_map/ppermute | solution.py:326
  9.3 5.6 %copy-start.3 = (bf16[4,128,512]{2,1,0:T(8,128)(2,1)S(1)}, bf16[4,128,512]{2,1,0:T(8,128)(2,1)}, u32[]{:S(2)}) copy-start(bf16[4,128,512]{2,1,0:T(8,128)(2,1)} %base.1) | copy-start | bytes 1572868
  9.4 5.6 %copy-start.8 = (bf16[512,512]{1,0:T(8,128)(2,1)S(1)}, bf16[512,512]{1,0:T(8,128)(2,1)}, u32[]{:S(2)}) copy-start(bf16[512,512]{1,0:T(8,128)(2,1)} %w_self.1) | copy-start | bytes 1572868
  9.4 5.6 %copy-start.9 = (bf16[4,4,128,128]{3,2,1,0:T(8,128)(2,1)S(1)}, bf16[4,4,128,128]{3,2,1,0:T(8,128)(2,1)}, u32[]{:S(2)}) copy-start(bf16[4,4,128,128]{3,2,1,0:T(8,128)(2,1)} %coupling.1) | copy-start | bytes 1572868
  9.4 5.6 %copy-start.10 = (s32[4,4]{1,0:T(4,128)S(1)}, s32[4,4]{1,0:T(4,128)}, u32[]{:S(2)}) copy-start(s32[4,4]{1,0:T(4,128)} %nbr.1) | copy-start | bytes 196
  9.4 5.6 %copy-start.11 = (f32[512]{0:T(512)S(1)}, f32[512]{0:T(512)}, u32[]{:S(2)}) copy-start(f32[512]{0:T(512)} %param.26) | copy-start | bytes 6148
  9.4 8.7 %collective-permute-start.1 = (bf16[2,128,512]{2,1,0:T(8,128)(2,1)S(1)}, bf16[2,128,512]{2,1,0:T(8,128)(2,1)S(1)}, u32[]{:S(2)}, u32[]{:S(2)}) collective-permute-start(bf16[2,128,512]{2,1,0:T(8,128)(2,1)S(1)} %pairs_off_late.1.refs_5_), channel_id=1, source_target_pairs={{0,15},{1,2},{2,1},{3,4},{4,3},{5,6},{6,5},{7,8},{8,7},{9,10},{10,... | collective-permute-start | bytes 786440 | tf_op jit(solution)/shard_map/ppermute | solution.py:326
  14.9 2.0 %collective-permute-start = (bf16[4,128,512]{2,1,0:T(8,128)(2,1)S(1)}, bf16[4,128,512]{2,1,0:T(8,128)(2,1)S(1)}, u32[]{:S(2)}, u32[]{:S(2)}) collective-permute-start(bf16[4,128,512]{2,1,0:T(8,128)(2,1)S(1)} %get-tuple-element.34), channel_id=1, source_target_pairs={{0,1},{1,0},{2,3},{3,2},{4,5},{5,4},{6,7},{7,6},{8,9},{9,8},{10,11... | collective-permute-start | bytes 1572872 | tf_op jit(solution)/shard_map/ppermute | solution.py:329
  15.0 1.8 %copy-start.4 = (bf16[512,512]{1,0:T(8,128)(2,1)S(1)}, bf16[512,512]{1,0:T(8,128)(2,1)}, u32[]{:S(2)}) copy-start(bf16[512,512]{1,0:T(8,128)(2,1)} %w_obs.1) | copy-start | bytes 1572868
  15.0 1.8 %copy-start.5 = (bf16[512,512]{1,0:T(8,128)(2,1)S(1)}, bf16[512,512]{1,0:T(8,128)(2,1)}, u32[]{:S(2)}) copy-start(bf16[512,512]{1,0:T(8,128)(2,1)} %w_out.1) | copy-start | bytes 1572868
  15.0 1.8 %copy-start.6 = (f32[2,512]{1,0:T(2,128)S(1)}, f32[2,512]{1,0:T(2,128)}, u32[]{:S(2)}) copy-start(f32[2,512]{1,0:T(2,128)} %gain.5) | copy-start | bytes 12292
  16.5 1.6 %copy-start.7 = (s32[1,2]{1,0:T(1,128)S(1)}, s32[1,2]{1,0:T(1,128)}, u32[]{:S(2)}) copy-start(s32[1,2]{1,0:T(1,128)} %rim_ref.3) | copy-start | bytes 28
  17.6 4.3 %copy-start = (bf16[2,512,512]{2,1,0:T(8,128)(2,1)S(1)}, bf16[2,512,512]{2,1,0:T(8,128)(2,1)}, u32[]{:S(2)}) copy-start(bf16[2,512,512]{2,1,0:T(8,128)(2,1)} %refs_2_.9) | copy-start | bytes 3145732
  18.1 8.6 %copy-start.1 = (bf16[2,512,512]{2,1,0:T(8,128)(2,1)S(1)}, bf16[2,512,512]{2,1,0:T(8,128)(2,1)}, u32[]{:S(2)}) copy-start(bf16[2,512,512]{2,1,0:T(8,128)(2,1)} %n_msg.5) | copy-start | bytes 3145732
  18.1 8.7 %copy-start.2 = (bf16[2,512,512]{2,1,0:T(8,128)(2,1)S(1)}, bf16[2,512,512]{2,1,0:T(8,128)(2,1)}, u32[]{:S(2)}) copy-start(bf16[2,512,512]{2,1,0:T(8,128)(2,1)} %n_out.5) | copy-start | bytes 3145732
  18.9 7.6 %collective-permute-start.5 = (bf16[128,640]{1,0:T(8,128)(2,1)S(1)}, bf16[128,640]{1,0:T(8,128)(2,1)S(1)}, u32[]{:S(2)}, u32[]{:S(2)}) collective-permute-start(bf16[128,640]{1,0:T(8,128)(2,1)S(1)} %get-tuple-element.42), channel_id=1, source_target_pairs={{0,15},{1,2},{2,1},{3,4},{4,3},{5,6},{6,5},{7,8},{8,7},{9,10},{10,... | collective-permute-start | bytes 491528 | tf_op jit(solution)/shard_map/ppermute | solution.py:326
  21.7 1.3 %collective-permute-start.3 = (bf16[128,512]{1,0:T(8,128)(2,1)S(1)}, bf16[128,512]{1,0:T(8,128)(2,1)S(1)}, u32[]{:S(2)}, u32[]{:S(2)}) collective-permute-start(bf16[128,512]{1,0:T(8,128)(2,1)S(1)} %get-tuple-element.40), channel_id=1, source_target_pairs={{0,1},{1,0},{2,3},{3,2},{4,5},{5,4},{6,7},{7,6},{8,9},{9,8},{10,11... | collective-permute-start | bytes 393224 | tf_op jit(solution)/shard_map/ppermute | solution.py:329
  23.2 7.2 %collective-permute-start.4 = (bf16[128,512]{1,0:T(8,128)(2,1)S(1)}, bf16[128,512]{1,0:T(8,128)(2,1)S(1)}, u32[]{:S(2)}, u32[]{:S(2)}) collective-permute-start(bf16[128,512]{1,0:T(8,128)(2,1)S(1)} %rim_message.1._), channel_id=1, source_target_pairs={{0,15},{1,2},{2,1},{3,4},{4,3},{5,6},{6,5},{7,8},{8,7},{9,10},{10,... | collective-permute-start | bytes 393224 | tf_op jit(solution)/shard_map/ppermute | solution.py:326
  28.0 3.0 %collective-permute-start.6 = (bf16[128,512]{1,0:T(8,128)(2,1)S(1)}, bf16[128,512]{1,0:T(8,128)(2,1)S(1)}, u32[]{:S(2)}, u32[]{:S(2)}) collective-permute-start(bf16[128,512]{1,0:T(8,128)(2,1)S(1)} %get-tuple-element.47._), channel_id=1, source_target_pairs={{0,1},{1,0},{2,3},{3,2},{4,5},{5,4},{6,7},{7,6},{8,9},{9,8},{10,11... | collective-permute-start | bytes 393224 | tf_op jit(solution)/shard_map/ppermute | solution.py:329
